TPU v7x, 32 devices: a whole 2x2x4 slice. The times are simulated.
32 devices in a mesh: dp: 8 (over z, x), expert: 4 (over y, core).
Axes of the slice: x: 2, y: 2, z: 4, core: 2. Of those that a mesh axis runs over, the one named last changes fastest.
Arguments:
- tokens: bfloat16 [25216, 768], P(('dp', 'expert')), may hold values from -6 to 6
- cotangent: bfloat16 [25216, 768], P(('dp', 'expert')), may hold values from -6 to 6
- bank_ids: int32 [128], P(('dp', 'expert')), may hold values from 0 to 7
- routes: int32 [25216, 2], P(('dp', 'expert')), may hold values from 0 to 7, all different within a row; in each aligned block of 788 rows (0 to 787, 788 to 1575, ...) at most 320 rows name the same one
- attn_gain: float32 [768], replicated, may hold values from 0.25 to 1.75
- expert_gain: float32 [768], replicated, may hold values from 0.25 to 1.75
- query_w: bfloat16 [768, 768], replicated, may hold values from -0.21875 to 0.21875
- key_w: bfloat16 [768, 768], replicated, may hold values from -0.21875 to 0.21875
- value_w: bfloat16 [768, 768], replicated, may hold values from -0.21875 to 0.21875
- out_w: bfloat16 [768, 768], replicated, may hold values from -0.875 to 0.875
- query_a: bfloat16 [768, 128], replicated, may hold values from -0.21875 to 0.21875
- query_b: bfloat16 [128, 768], replicated, may hold values from -1.5 to 1.5
- key_a: bfloat16 [768, 128], replicated, may hold values from -0.21875 to 0.21875
- key_b: bfloat16 [128, 768], replicated, may hold values from -1.5 to 1.5
- value_a: bfloat16 [768, 128], replicated, may hold values from -0.21875 to 0.21875
- value_b: bfloat16 [128, 768], replicated, may hold values from -1.5 to 1.5
- out_a: bfloat16 [768, 128], replicated, may hold values from -0.875 to 0.875
- out_b: bfloat16 [128, 768], replicated, may hold values from -1.5 to 1.5
- router_w: bfloat16 [768, 8], replicated, may hold values from -0.099609375 to 0.099609375
- router_a: bfloat16 [768, 128], replicated, may hold values from -0.21875 to 0.21875
- router_b: bfloat16 [128, 8], replicated, may hold values from -0.75 to 0.75
- up_w: bfloat16 [8, 768, 3072], P('expert'), may hold values from -0.21875 to 0.21875
- up_a: bfloat16 [8, 768, 128], P('expert'), may hold values from -0.21875 to 0.21875
- up_b: bfloat16 [8, 128, 3072], P('expert'), may hold values from -1.5 to 1.5
- down_w: bfloat16 [8, 3072, 768], P('expert'), may hold values from -0.4375 to 0.4375
- down_a: bfloat16 [8, 3072, 128], P('expert'), may hold values from -0.4375 to 0.4375
- down_b: bfloat16 [8, 128, 768], P('expert'), may hold values from -1.5 to 1.5
Outputs:
- mixed: bfloat16 [25216, 768], P(('dp', 'expert'))
- input_grad: float32 [25216, 768], P(('dp', 'expert'))
- query_a_grad: float32 [768, 128], replicated
- query_b_grad: float32 [128, 768], replicated
- key_a_grad: float32 [768, 128], replicated
- key_b_grad: float32 [128, 768], replicated
- value_a_grad: float32 [768, 128], replicated
- value_b_grad: float32 [128, 768], replicated
- out_a_grad: float32 [768, 128], replicated
- out_b_grad: float32 [128, 768], replicated
- router_a_grad: float32 [768, 128], replicated
- router_b_grad: float32 [128, 8], replicated
- up_a_grad: float32 [8, 768, 128], P('expert')
- up_b_grad: float32 [8, 128, 3072], P('expert')
- down_a_grad: float32 [8, 3072, 128], P('expert')
- down_b_grad: float32 [8, 128, 768], P('expert')
Inputs may be any that keep to these rules, and one draw needn't show every extreme that they name: `routes`: the two experts of a row differ and every expert is named by some row. In the 788 rows of one device no expert is named by more than 320 rows, and in some device's rows one expert is named by exactly 320.
All inputs are finite; a program needn't handle non-finite values.
Results may differ from a plain program's by a relative error of at most 0.018.
The roundings to bfloat16 on the way count: a program that leaves them out, or rounds other values in their place, can miss the bound.
Values may be sent and summed in bfloat16 or wider, within the bound.
No kernel may reach another device: no remote copies, remote signals or barrier semaphores. Data moves between devices by JAX's collectives and lax.ppermute only.
A program may use at most 256 MiB of HBM per device.

v0:
```python
import jax
import jax.numpy as jnp
from jax import lax
from jax.sharding import PartitionSpec as P

HEADS = 12
HEAD_DIM = 64
RANK = 16
SEQ = 197


EPSILON = 1e-06


def layer_norm(values, norm_gain):
    average = jnp.mean(values, axis=-1, keepdims=True)
    centred = values - average
    spread = jnp.mean(centred * centred, axis=-1, keepdims=True)
    return norm_gain * centred * lax.rsqrt(spread + EPSILON)


def norm_backward(values, norm_gain, gradient):
    _, pullback = jax.vjp(lambda inside: layer_norm(inside, norm_gain), values)
    return pullback(gradient)[0]


def smooth_gate(values):
    return jax.nn.gelu(values, approximate=False)


def product(first_op, second_op):
    return jnp.dot(first_op, second_op, preferred_element_type=jnp.float32)


def product_tn(first_op, second_op):
    return lax.dot_general(
        first_op, second_op, (((0,), (0,)), ((), ())), preferred_element_type=jnp.float32
    )


def product_nt(first_op, second_op):
    return lax.dot_general(
        first_op, second_op, (((1,), (1,)), ((), ())), preferred_element_type=jnp.float32
    )


def bank_columns(row_banks, columns):
    column_bank = lax.broadcasted_iota(jnp.int32, (row_banks.shape[0], columns), 1) // RANK
    return (column_bank == row_banks[:, None]).astype(jnp.float32)


def adapted_forward(row_block, weight, down_proj, up_proj, bank_cols):
    low_rank = (product(row_block, down_proj) * bank_cols).astype(jnp.bfloat16)
    return (product(row_block, weight) + product(low_rank, up_proj), low_rank)


def adapted_backward(row_block, low_rank, gradient, weight, down_proj, up_proj, bank_cols):
    grad_up = product_tn(low_rank, gradient)
    grad_low = (product_nt(gradient, up_proj) * bank_cols).astype(jnp.bfloat16)
    grad_down = product_tn(row_block, grad_low)
    grad_rows = product_nt(gradient, weight) + product_nt(grad_low, down_proj)
    return (grad_rows, grad_down, grad_up)


def head_split(row_block):
    return row_block.reshape(-1, SEQ, HEADS, HEAD_DIM)


def attention_scores(query_h, key_h):
    return jnp.einsum(
        "bqhd,bkhd->bhqk", query_h, key_h, preferred_element_type=jnp.float32
    ) * HEAD_DIM ** (-0.5)


def route_slots(flat_routes, experts, capacity):
    count = flat_routes.shape[0]
    expert_ids = lax.broadcasted_iota(jnp.int32, (count, experts), 1)
    onehot = (flat_routes[:, None] == expert_ids).astype(jnp.int32)
    before = jnp.cumsum(onehot, axis=0) - onehot
    position = jnp.sum(before * onehot, axis=1)
    slot_index = flat_routes * capacity + position
    route_index = jnp.full((experts * capacity,), count, jnp.int32)
    route_index = route_index.at[slot_index].set(jnp.arange(count, dtype=jnp.int32))
    return (slot_index, route_index)


def expert_inside(row_block, bank_cols, up_weight, up_first, up_second, down_first):
    pre_act, low_up = adapted_forward(row_block, up_weight, up_first, up_second, bank_cols)
    hidden = smooth_gate(pre_act).astype(jnp.bfloat16)
    low_down = (product(hidden, down_first) * bank_cols).astype(jnp.bfloat16)
    return (pre_act, low_up, hidden, low_down)


def experts_forward(recv_rows, recv_banks, up_w, up_a, up_b, down_w, down_a, down_b, capacity):
    groups = recv_rows.shape[0]
    local_experts = up_w.shape[0]
    model_width = recv_rows.shape[2]
    adapter_width = up_a.shape[2]
    recv_rows = recv_rows.reshape(groups, local_experts, capacity, model_width)
    recv_banks = recv_banks.astype(jnp.int32).reshape(groups, local_experts, capacity)
    expert_rows = []
    expert_cols = []
    kept_parts = []
    results = []
    for expert_id in range(local_experts):
        row_block = recv_rows[:, expert_id].reshape(groups * capacity, model_width)
        bank_cols = bank_columns(recv_banks[:, expert_id].reshape(-1), adapter_width)
        inside = expert_inside(
            row_block,
            bank_cols,
            up_w[expert_id],
            up_a[expert_id],
            up_b[expert_id],
            down_a[expert_id],
        )
        result = product(inside[2], down_w[expert_id]) + product(inside[3], down_b[expert_id])
        expert_rows.append(row_block)
        expert_cols.append(bank_cols)
        kept_parts.append(inside)
        results.append(result.astype(jnp.bfloat16).reshape(groups, capacity, model_width))
    out_send = jnp.stack(results, axis=1).reshape(groups, local_experts * capacity, model_width)
    return (expert_rows, expert_cols, kept_parts, out_send)


def experts_backward(
    recv_grads,
    expert_rows,
    expert_cols,
    kept_parts,
    up_w,
    up_a,
    up_b,
    down_w,
    down_a,
    down_b,
    capacity,
):
    groups = recv_grads.shape[0]
    local_experts = up_w.shape[0]
    model_width = recv_grads.shape[2]
    recv_grads = recv_grads.reshape(groups, local_experts, capacity, model_width)
    grads_up_a = []
    grads_up_b = []
    grads_down_a = []
    grads_down_b = []
    row_grads = []
    for expert_id in range(local_experts):
        row_block = expert_rows[expert_id]
        bank_cols = expert_cols[expert_id]
        pre_act, low_up, hidden, low_down = kept_parts[expert_id]
        grad_block = recv_grads[:, expert_id].reshape(groups * capacity, model_width)
        grad_hidden, grad_down_a, grad_down_b = adapted_backward(
            hidden,
            low_down,
            grad_block,
            down_w[expert_id],
            down_a[expert_id],
            down_b[expert_id],
            bank_cols,
        )
        _, gate_pull = jax.vjp(smooth_gate, pre_act)
        grad_pre = gate_pull(grad_hidden)[0].astype(jnp.bfloat16)
        grad_block_rows, grad_up_a, grad_up_b = adapted_backward(
            row_block,
            low_up,
            grad_pre,
            up_w[expert_id],
            up_a[expert_id],
            up_b[expert_id],
            bank_cols,
        )
        grads_up_a.append(grad_up_a)
        grads_up_b.append(grad_up_b)
        grads_down_a.append(grad_down_a)
        grads_down_b.append(grad_down_b)
        row_grads.append(
            grad_block_rows.astype(jnp.bfloat16).reshape(groups, capacity, model_width)
        )
    grad_send = jnp.stack(row_grads, axis=1).reshape(groups, local_experts * capacity, model_width)
    return (
        grad_send,
        jnp.stack(grads_up_a, axis=0),
        jnp.stack(grads_up_b, axis=0),
        jnp.stack(grads_down_a, axis=0),
        jnp.stack(grads_down_b, axis=0),
    )


def body(
    tokens,
    cotangent,
    bank_ids,
    routes,
    attn_gain,
    expert_gain,
    query_w,
    key_w,
    value_w,
    out_w,
    query_a,
    query_b,
    key_a,
    key_b,
    value_a,
    value_b,
    out_a,
    out_b,
    router_w,
    router_a,
    router_b,
    up_w,
    up_a,
    up_b,
    down_w,
    down_a,
    down_b,
):
    row_count = tokens.shape[0]
    model_width = tokens.shape[1]
    adapter_width = query_a.shape[1]
    local_experts = up_w.shape[0]
    groups = lax.axis_size("expert")
    experts = local_experts * groups
    capacity = 13 * row_count // (4 * experts)
    token_banks = jnp.repeat(bank_ids, SEQ)
    token_cols = bank_columns(token_banks, adapter_width)
    tokens_wide = tokens.astype(jnp.float32)
    normed_one = layer_norm(tokens_wide, attn_gain).astype(jnp.bfloat16)
    query_full, query_low = adapted_forward(normed_one, query_w, query_a, query_b, token_cols)
    key_full, key_low = adapted_forward(normed_one, key_w, key_a, key_b, token_cols)
    value_full, value_low = adapted_forward(normed_one, value_w, value_a, value_b, token_cols)
    query_h = head_split(query_full.astype(jnp.bfloat16))
    key_h = head_split(key_full.astype(jnp.bfloat16))
    value_h = head_split(value_full.astype(jnp.bfloat16))
    scores = attention_scores(query_h, key_h)
    top_score = jnp.max(scores, axis=-1, keepdims=True)
    shifted = jnp.exp(scores - top_score)
    denominator = jnp.sum(shifted, axis=-1, keepdims=True)
    log_total = top_score + jnp.log(denominator)
    weights_low = (shifted / denominator).astype(jnp.bfloat16)
    attended = jnp.einsum(
        "bhqk,bkhd->bqhd", weights_low, value_h, preferred_element_type=jnp.float32
    )
    attended_low = attended.reshape(row_count, model_width).astype(jnp.bfloat16)
    attn_result, out_low = adapted_forward(attended_low, out_w, out_a, out_b, token_cols)
    mid_sum = tokens_wide + attn_result
    normed_two = layer_norm(mid_sum, expert_gain).astype(jnp.bfloat16)
    logits, router_low = adapted_forward(normed_two, router_w, router_a, router_b, token_cols)
    router_probs = jax.nn.softmax(logits, axis=-1)
    expert_ids = lax.broadcasted_iota(jnp.int32, (row_count, 2, experts), 2)
    route_match = routes[:, :, None] == expert_ids
    gate_values = jnp.sum(jnp.where(route_match, router_probs[:, None, :], 0.0), axis=2)
    flat_routes = routes.reshape(-1)
    slot_index, route_index = route_slots(flat_routes, experts, capacity)
    token_index = route_index // 2
    padded_rows = jnp.concatenate([normed_two, jnp.zeros((1, model_width), jnp.bfloat16)], axis=0)
    padded_banks = jnp.concatenate([token_banks, jnp.zeros((1,), jnp.int32)])
    send_rows = padded_rows[token_index].reshape(groups, local_experts * capacity, model_width)
    send_banks = (
        padded_banks[token_index].astype(jnp.bfloat16).reshape(groups, local_experts * capacity)
    )
    grad_out = cotangent.astype(jnp.float32)
    grad_routes = (
        (gate_values[:, :, None] * grad_out[:, None, :])
        .astype(jnp.bfloat16)
        .reshape(2 * row_count, model_width)
    )
    padded_grads = jnp.concatenate([grad_routes, jnp.zeros((1, model_width), jnp.bfloat16)], axis=0)
    send_grads = padded_grads[route_index].reshape(groups, local_experts * capacity, model_width)
    recv_rows, recv_banks = (
        lax.all_to_all(send_rows, "expert", split_axis=0, concat_axis=0, tiled=True),
        lax.all_to_all(send_banks, "expert", split_axis=0, concat_axis=0, tiled=True),
    )
    expert_rows, expert_cols, kept_parts, out_send = experts_forward(
        recv_rows, recv_banks, up_w, up_a, up_b, down_w, down_a, down_b, capacity
    )
    back_rows = lax.all_to_all(out_send, "expert", split_axis=0, concat_axis=0, tiled=True)
    recv_grads = lax.all_to_all(send_grads, "expert", split_axis=0, concat_axis=0, tiled=True)
    grad_send, up_a_grad, up_b_grad, down_a_grad, down_b_grad = experts_backward(
        recv_grads,
        expert_rows,
        expert_cols,
        kept_parts,
        up_w,
        up_a,
        up_b,
        down_w,
        down_a,
        down_b,
        capacity,
    )
    grad_back = lax.all_to_all(grad_send, "expert", split_axis=0, concat_axis=0, tiled=True)
    returned = back_rows.reshape(experts * capacity, model_width)[slot_index].reshape(
        row_count, 2, model_width
    )
    returned_wide = returned.astype(jnp.float32)
    mixed_out = mid_sum + jnp.sum(gate_values[:, :, None] * returned_wide, axis=1)
    grad_gates = jnp.sum(grad_out[:, None, :] * returned_wide, axis=2)
    from_experts = grad_back.reshape(experts * capacity, model_width)[slot_index].reshape(
        row_count, 2, model_width
    )
    grad_probs = jnp.sum(jnp.where(route_match, grad_gates[:, :, None], 0.0), axis=1)
    grad_logits = (
        router_probs * (grad_probs - jnp.sum(grad_probs * router_probs, axis=1, keepdims=True))
    ).astype(jnp.bfloat16)
    grad_norm_two, router_a_grad, router_b_grad = adapted_backward(
        normed_two, router_low, grad_logits, router_w, router_a, router_b, token_cols
    )
    grad_norm_two = grad_norm_two + jnp.sum(from_experts.astype(jnp.float32), axis=1)
    grad_mid = grad_out + norm_backward(mid_sum, expert_gain, grad_norm_two)
    grad_mid_low = grad_mid.astype(jnp.bfloat16)
    grad_attended, out_a_grad, out_b_grad = adapted_backward(
        attended_low, out_low, grad_mid_low, out_w, out_a, out_b, token_cols
    )
    grad_att_h = head_split(grad_attended.astype(jnp.bfloat16))
    probs_again = jnp.exp(attention_scores(query_h, key_h) - log_total)
    weights_again = probs_again.astype(jnp.bfloat16)
    grad_weights = jnp.einsum(
        "bqhd,bkhd->bhqk", grad_att_h, value_h, preferred_element_type=jnp.float32
    )
    grad_scores = (
        probs_again * (grad_weights - jnp.sum(grad_weights * probs_again, axis=-1, keepdims=True))
    ).astype(jnp.bfloat16)
    grad_query = jnp.einsum(
        "bhqk,bkhd->bqhd", grad_scores, key_h, preferred_element_type=jnp.float32
    ) * HEAD_DIM ** (-0.5)
    grad_key = jnp.einsum(
        "bhqk,bqhd->bkhd", grad_scores, query_h, preferred_element_type=jnp.float32
    ) * HEAD_DIM ** (-0.5)
    grad_value = jnp.einsum(
        "bhqk,bqhd->bkhd", weights_again, grad_att_h, preferred_element_type=jnp.float32
    )
    grad_query = grad_query.reshape(row_count, model_width).astype(jnp.bfloat16)
    grad_key = grad_key.reshape(row_count, model_width).astype(jnp.bfloat16)
    grad_value = grad_value.reshape(row_count, model_width).astype(jnp.bfloat16)
    from_query, query_a_grad, query_b_grad = adapted_backward(
        normed_one, query_low, grad_query, query_w, query_a, query_b, token_cols
    )
    from_key, key_a_grad, key_b_grad = adapted_backward(
        normed_one, key_low, grad_key, key_w, key_a, key_b, token_cols
    )
    from_value, value_a_grad, value_b_grad = adapted_backward(
        normed_one, value_low, grad_value, value_w, value_a, value_b, token_cols
    )
    grad_norm_one = from_query + from_key + from_value
    input_grad = grad_mid + norm_backward(tokens_wide, attn_gain, grad_norm_one)
    (
        query_a_grad,
        query_b_grad,
        key_a_grad,
        key_b_grad,
        value_a_grad,
        value_b_grad,
        out_a_grad,
        out_b_grad,
        router_a_grad,
        router_b_grad,
    ) = lax.psum(
        (
            query_a_grad,
            query_b_grad,
            key_a_grad,
            key_b_grad,
            value_a_grad,
            value_b_grad,
            out_a_grad,
            out_b_grad,
            router_a_grad,
            router_b_grad,
        ),
        ("dp", "expert"),
    )
    up_a_grad, up_b_grad, down_a_grad, down_b_grad = lax.psum(
        (up_a_grad, up_b_grad, down_a_grad, down_b_grad), "dp"
    )
    return (
        mixed_out.astype(jnp.bfloat16),
        input_grad,
        query_a_grad,
        query_b_grad,
        key_a_grad,
        key_b_grad,
        value_a_grad,
        value_b_grad,
        out_a_grad,
        out_b_grad,
        router_a_grad,
        router_b_grad,
        up_a_grad,
        up_b_grad,
        down_a_grad,
        down_b_grad,
    )


def solution(mesh):
    in_specs = (
        P(("dp", "expert"), None),
        P(("dp", "expert"), None),
        P(("dp", "expert")),
        P(("dp", "expert"), None),
        P(),
        P(),
        P(),
        P(),
        P(),
        P(),
        P(),
        P(),
        P(),
        P(),
        P(),
        P(),
        P(),
        P(),
        P(),
        P(),
        P(),
        P("expert", None, None),
        P("expert", None, None),
        P("expert", None, None),
        P("expert", None, None),
        P("expert", None, None),
        P("expert", None, None),
    )
    out_specs = (
        P(("dp", "expert"), None),
        P(("dp", "expert"), None),
        P(),
        P(),
        P(),
        P(),
        P(),
        P(),
        P(),
        P(),
        P(),
        P(),
        P("expert", None, None),
        P("expert", None, None),
        P("expert", None, None),
        P("expert", None, None),
    )
    return jax.shard_map(body, mesh=mesh, in_specs=in_specs, out_specs=out_specs, check_vma=False)
```

profile of v0, /device:TPU:0, one launch (start us, length us, event | category | flops | bytes accessed | tf_op | source)
XLA Modules:
  0.0 1104.8 jit_solution(16518576930097699462)
XLA Ops:
  13.4 8.8 scatter_custom_fusion
  22.3 9.4 gather_fusion.1
  43.3 4.8 reshape.298
  48.1 4.9 copy.151
  58.6 4.8 reshape.299
  63.4 4.9 copy.149
  73.8 4.8 reshape.300
  78.6 5.3 copy.150
  107.1 8.6 gather_fusion
  115.7 5.1 all-to-all-start
  124.4 7.2 mul.340
  138.2 12.3 %gather_fusion.3 = bf16[2560,768]{1,0:T(8,128)(2,1)} fusion(bf16[1577,768]{1,0:T(8,128)(2,1)} %concatenate.11, s32[3072]{0:T(1024)S(1)} %get-tuple-element.62), kind=kCustom, calls=%fused_computation.3 | custom fusion | bytes 7874560 | tf_op jit(solution)/shard_map/gather | solution.py:269
  150.5 15.8 %all-to-all-done = bf16[4,640,768]{2,1,0:T(8,128)(2,1)} async-done(((bf16[4,640,768]{2,1,0:T(8,128)(2,1)}), bf16[4,640,768]{2,1,0:T(8,128)(2,1)}, u32[]{:S(2)}, u32[]{:S(2)}) %all-to-all-start) | async-done | bytes 3932192 | tf_op jit(solution)/shard_map/all_to_all | solution.py:271
  166.2 4.8 all-to-all-start.3
  175.7 40.7 %all-to-all-done.3 = bf16[4,640,768]{2,1,0:T(8,128)(2,1)} async-done(((bf16[4,640,768]{2,1,0:T(8,128)(2,1)}), bf16[4,640,768]{2,1,0:T(8,128)(2,1)}, u32[]{:S(2)}, u32[]{:S(2)}) %all-to-all-start.3) | async-done | bytes 3932192 | tf_op jit(solution)/shard_map/all_to_all | solution.py:278
  220.3 12.7 %fusion.25 = f32[1280,3072]{1,0:T(8,128)} fusion(bf16[1280,768]{1,0:T(8,128)(2,1)S(1)} %bitcast.272, bf16[2,768,3072]{2,1,0:T(8,128)(2,1)} %param.48), kind=kOutput, calls=%fused_computation.63 | convolution fusion | flops 6039797760 | bytes 22413312 | tf_op jit(solution)/shard_map/dot_general | solution.py:32
  233.8 9.3 fusion.19
  244.5 39.5 %multiply_convert_fusion = (bf16[1280,3072]{1,0:T(8,128)(2,1)}, f32[1280,3072]{1,0:T(8,128)}, f32[1280,3072]{1,0:T(8,128)}) fusion(f32[1280,3072]{1,0:T(8,128)} %fusion.25, bf16[1280,128]{1,0:T(8,128)(2,1)S(1)} %fusion.60, bf16[2,128,3072]{2,1,0:T(8,128)(2,1)S(1)} %copy-done.141), kind=kOutput, calls=%fused_computation.12 | convolution fusion | flops 1266155520 | bytes 56164352 | tf_op jit(solution)/shard_map/dot_general | solution.py:32
  284.0 18.0 %add_convert_fusion = bf16[1280,3072]{1,0:T(8,128)(2,1)S(1)} fusion(f32[1280,3072]{1,0:T(8,128)} %get-tuple-element.38, f32[1280,3072]{1,0:T(8,128)} %fusion.19, f32[1280,3072]{1,0:T(8,128)} %get-tuple-element.50, bf16[1280,128]{1,0:T(8,128)(2,1)S(1)} %fusion.62, bf16[2,3072,128]{2,1,0:T(8,128)(2,1)} %param.52), kind=kOutput, calls=%fused_computation.10 | convolution fusion | flops 1065615360 | bytes 56164352 | tf_op jit(solution)/shard_map/dot_general | solution.py:42
  302.0 13.4 %fusion.23 = f32[1280,768]{1,0:T(8,128)} fusion(bf16[1280,3072]{1,0:T(8,128)(2,1)S(1)} %add_convert_fusion, bf16[2,768,3072]{2,1,0:T(8,128)(2,1)} %param.48), kind=kOutput, calls=%fused_computation.61 | convolution fusion | flops 6039797760 | bytes 16515072 | tf_op jit(solution)/shard_map/dot_general | solution.py:42
  318.4 12.2 %fusion.33 = f32[1280,3072]{1,0:T(8,128)} fusion(bf16[1280,768]{1,0:T(8,128)(2,1)S(1)} %bitcast.269, bf16[2,768,3072]{2,1,0:T(8,128)(2,1)} %param.48), kind=kOutput, calls=%fused_computation.71 | convolution fusion | flops 6039797760 | bytes 22413312 | tf_op jit(solution)/shard_map/dot_general | solution.py:32
  332.1 9.2 fusion.27
  342.0 39.5 %multiply_convert_fusion.1 = (bf16[1280,3072]{1,0:T(8,128)(2,1)}, f32[1280,3072]{1,0:T(8,128)}, f32[1280,3072]{1,0:T(8,128)}) fusion(f32[1280,3072]{1,0:T(8,128)} %fusion.33, bf16[1280,128]{1,0:T(8,128)(2,1)S(1)} %fusion.59, bf16[2,128,3072]{2,1,0:T(8,128)(2,1)S(1)} %copy-done.141), kind=kOutput, calls=%fused_computation.25 | convolution fusion | flops 1266155520 | bytes 56164352 | tf_op jit(solution)/shard_map/dot_general | solution.py:32
  381.6 17.7 %add_convert_fusion.1 = bf16[1280,3072]{1,0:T(8,128)(2,1)S(1)} fusion(f32[1280,3072]{1,0:T(8,128)} %get-tuple-element.36, f32[1280,3072]{1,0:T(8,128)} %fusion.27, f32[1280,3072]{1,0:T(8,128)} %get-tuple-element.53, bf16[1280,128]{1,0:T(8,128)(2,1)S(1)} %fusion.61, bf16[2,3072,128]{2,1,0:T(8,128)(2,1)} %param.52), kind=kOutput, calls=%fused_computation.11 | convolution fusion | flops 1065615360 | bytes 56164352 | tf_op jit(solution)/shard_map/dot_general | solution.py:42
  399.3 11.6 %fusion.31 = f32[1280,768]{1,0:T(8,128)S(1)} fusion(bf16[1280,3072]{1,0:T(8,128)(2,1)S(1)} %add_convert_fusion.1, bf16[2,768,3072]{2,1,0:T(8,128)(2,1)} %param.48), kind=kOutput, calls=%fused_computation.69 | convolution fusion | flops 6039797760 | bytes 16515072 | tf_op jit(solution)/shard_map/dot_general | solution.py:42
  414.2 10.6 fusion.21
  431.1 4.8 all-to-all-start.4
  435.9 5.7 fusion.55
  442.3 10.0 fusion.29
  455.2 26.1 %all-to-all-done.4 = bf16[4,640,768]{2,1,0:T(8,128)(2,1)} async-done(((bf16[4,640,768]{2,1,0:T(8,128)(2,1)}), bf16[4,640,768]{2,1,0:T(8,128)(2,1)}, u32[]{:S(2)}, u32[]{:S(2)}) %all-to-all-start.4) | async-done | bytes 3932192 | tf_op jit(solution)/shard_map/all_to_all | solution.py:292
  481.3 4.9 all-to-all-start.2
  503.9 10.1 gather_fusion.4
  514.0 6.4 reshape.246
  520.4 11.2 %all-to-all-done.2 = bf16[4,640,768]{2,1,0:T(8,128)(2,1)} async-done(((bf16[4,640,768]{2,1,0:T(8,128)(2,1)}), bf16[4,640,768]{2,1,0:T(8,128)(2,1)}, u32[]{:S(2)}, u32[]{:S(2)}) %all-to-all-start.2) | async-done | bytes 3932192 | tf_op jit(solution)/shard_map/all_to_all | solution.py:277
  531.7 10.1 gather_fusion.2
  541.8 6.5 reshape.245
  548.3 14.1 %multiply_reduce_fusion.2 = (f32[788,2]{1,0:T(8,128)S(1)}, f32[788,768]{1,0:T(8,128)}) fusion(f32[788,2,768]{2,1,0:T(2,128)} %reshape.245, f32[788,768]{1,0:T(8,128)} %convert_element_type.235, f32[788,2]{1,0:T(8,128)S(1)} %copy-done.44), kind=kLoop, calls=%fused_computation.55 | loop fusion | flops 4234712 | bytes 9695552 | tf_op jit(solution)/shard_map/reduce_sum | solution.py:298
  566.1 9.6 reduce_sum.209
  591.0 5.0 copy.166
  596.1 7.5 fusion.67
  603.6 7.5 multiply_reduce_fusion
  611.2 11.5 %multiply_convert_fusion.2 = bf16[4,12,197,197]{2,3,1,0:T(8,128)(2,1)} fusion(f32[4,12,197,197]{2,3,1,0:T(8,128)} %get-tuple-element.57, f32[4,12,197,197]{2,3,1,0:T(8,128)} %copy-done.1, f32[4,12,197]{2,1,0:T(8,128)S(1)} %get-tuple-element.56, f32[4,12,197]{2,1,0:T(8,128)S(1)} %log_add_fusion), kind=kLoop, calls=%fused_computation.42 | loop fusion | flops 9314160 | bytes 18703968 | tf_op jit(solution)/shard_map/convert_element_type | solution.py:323
  622.7 5.8 fusion.72
  676.5 5.6 convolution_bitcast_fusion
  682.1 5.6 convolution_bitcast_fusion.1
  690.7 40.4 %psum.107 = f32[128,8]{0,1:T(8,128)} all-reduce(f32[128,8]{0,1:T(8,128)S(1)} %fusion.158), channel_id=1, replica_groups=mesh['dp'=8,'expert'=4] {'dp','expert'}, use_global_device_ids=true, to_apply=%region_32.33 | all-reduce | flops 1024 | bytes 8192 | tf_op jit(solution)/shard_map/psum | solution.py:358
  744.5 73.4 %all-reduce.8.cloned.1.call-done = (f32[768,128]{1,0:T(8,128)}, f32[128,768]{1,0:T(8,128)}, f32[768,128]{1,0:T(8,128)}, f32[128,768]{1,0:T(8,128)}, f32[768,128]...) async-done(((f32[768,128]{1,0:T(8,128)}, f32[128,768]{1,0:T(8,128)}, f32[768,128]{1,0:T(8,128)}, ...) | async-done | bytes 3538960 | tf_op jit(solution)/shard_map/psum | solution.py:358
  817.9 262.4 %all-reduce.10.cloned.1.call-done = (f32[2,768,128]{2,1,0:T(8,128)}, f32[2,128,3072]{2,1,0:T(8,128)}, f32[2,3072,128]{2,1,0:T(8,128)}, f32[2,128,768]{2,1,0:T(8,128)}) async-done(((f32[2,768,128]{2,1,0:T(8,128)}, f32[2,128,3072]{2,1,0:T(8,128)}, f32[2,3072,128]{2,1,0:T(8,128)}, f32[2,128,768]{2,1,0:T(8,128)}), (f32[2,768,128]{2,1,0:T(8,128)}, f32[2,128,3072]{2,1,0:T(8,128)}, f32[2,3072,128]{2,1,0:T(8,128)}, ...) | async-done | bytes 7864336 | tf_op jit(solution)/shard_map/psum | solution.py:373
  (484 shorter events, 208.5 us)
Async XLA Ops:
  7.2 93.1 %copy-start = (bf16[768,768]{1,0:T(8,128)(2,1)S(1)}, bf16[768,768]{1,0:T(8,128)(2,1)}, u32[]{:S(2)}) copy-start(bf16[768,768]{1,0:T(8,128)(2,1)} %param.36) | copy-start | bytes 3538948
  9.7 122.3 %copy-start.134 = (s32[788]{0:T(1024)}, s32[788]{0:T(1024)S(1)}, u32[]{:S(2)}) copy-start(s32[788]{0:T(1024)S(1)} %eq.53) | copy-start | bytes 9460
  22.3 15.8 %copy-start.4 = (bf16[788,768]{1,0:T(8,128)(2,1)S(1)}, bf16[788,768]{1,0:T(8,128)(2,1)}, u32[]{:S(2)}) copy-start(bf16[788,768]{1,0:T(8,128)(2,1)} %param.27) | copy-start | bytes 3631108
  22.3 16.7 %copy-start.116 = (f32[768]{0:T(1024)S(1)}, f32[768]{0:T(1024)}, u32[]{:S(2)}) copy-start(f32[768]{0:T(1024)} %param.31) | copy-start | bytes 9220
  33.6 82.1 %all-to-all-start.1 = ((bf16[4,2,320]{2,1,0:T(2,128)(2,1)}), bf16[4,2,320]{2,1,0:T(2,128)(2,1)S(1)}, u32[]{:S(2)}, u32[]{:S(2)}) async-start(bf16[4,2,320]{2,1,0:T(2,128)(2,1)} %reshape.309), calls=%async_computation.1 | async-start | bytes 12288 | tf_op jit(solution)/shard_map/all_to_all | solution.py:272
  104.7 11.0 copy-start.130
  115.7 50.5 %all-to-all-start = ((bf16[4,640,768]{2,1,0:T(8,128)(2,1)}), bf16[4,640,768]{2,1,0:T(8,128)(2,1)}, u32[]{:S(2)}, u32[]{:S(2)}) async-start(bf16[4,640,768]{2,1,0:T(8,128)(2,1)} %bitcast.266), calls=%async_computation | async-start | bytes 7864320 | tf_op jit(solution)/shard_map/all_to_all | solution.py:271
  166.2 50.2 %all-to-all-start.3 = ((bf16[4,640,768]{2,1,0:T(8,128)(2,1)}), bf16[4,640,768]{2,1,0:T(8,128)(2,1)}, u32[]{:S(2)}, u32[]{:S(2)}) async-start(bf16[4,640,768]{2,1,0:T(8,128)(2,1)} %bitcast.267), calls=%async_computation.3 | async-start | bytes 7864320 | tf_op jit(solution)/shard_map/all_to_all | solution.py:278
  171.4 144.0 %copy-start.137 = (s32[1280]{0:T(1024)}, s32[1280]{0:T(1024)S(1)}, u32[]{:S(2)}) copy-start(s32[1280]{0:T(1024)S(1)} %eq.66) | copy-start | bytes 15364
  175.7 57.3 %copy-start.24 = (bf16[4,1,320,768]{3,2,1,0:T(8,128)(2,1)}, bf16[4,1,320,768]{3,2,1,0:T(8,128)(2,1)S(1)}, u32[]{:S(2)}) copy-start(bf16[4,1,320,768]{3,2,1,0:T(8,128)(2,1)S(1)} %get-tuple-element.42) | copy-start | bytes 5898244
  216.5 17.3 %slice-start.4 = ((s8[9437184]{0:T(1024)(128)(4,1)}), s8[4194304]{0:T(1024)(128)(4,1)S(1)}, s32[]{:S(2)}) async-start(s8[9437184]{0:T(1024)(128)(4,1)} %bitcast.287), calls=%async_computation.11 | async-start | bytes 8388608
  220.3 22.8 %copy-start.29 = (bf16[4,1,320,768]{3,2,1,0:T(8,128)(2,1)}, bf16[4,1,320,768]{3,2,1,0:T(8,128)(2,1)S(1)}, u32[]{:S(2)}) copy-start(bf16[4,1,320,768]{3,2,1,0:T(8,128)(2,1)S(1)} %get-tuple-element.40) | copy-start | bytes 5898244
  220.3 12.7 %copy-start.78 = (bf16[2,768,128]{2,1,0:T(8,128)(2,1)S(1)}, bf16[2,768,128]{2,1,0:T(8,128)(2,1)}, u32[]{:S(2)}) copy-start(bf16[2,768,128]{2,1,0:T(8,128)(2,1)} %param.49) | copy-start | bytes 1179652
  220.3 13.4 %slice-start.5 = ((s8[9437184]{0:T(1024)(128)(4,1)}), s8[4194304]{0:T(1024)(128)(4,1)S(1)}, s32[]{:S(2)}) async-start(s8[9437184]{0:T(1024)(128)(4,1)} %bitcast.287), calls=%async_computation.12 | async-start | bytes 8388608
  220.3 13.5 %slice-start.6 = ((s8[9437184]{0:T(1024)(128)(4,1)}), s8[1048576]{0:T(1024)(128)(4,1)S(1)}, s32[]{:S(2)}) async-start(s8[9437184]{0:T(1024)(128)(4,1)} %bitcast.287), calls=%async_computation.13 | async-start | bytes 2097152
  244.5 39.5 %copy-start.89 = (bf16[1280,128]{1,0:T(8,128)(2,1)}, bf16[1280,128]{1,0:T(8,128)(2,1)S(1)}, u32[]{:S(2)}) copy-start(bf16[1280,128]{1,0:T(8,128)(2,1)S(1)} %fusion.62) | copy-start | bytes 983044
  302.0 13.4 %copy-start.9 = (bf16[1280,3072]{1,0:T(8,128)(2,1)}, bf16[1280,3072]{1,0:T(8,128)(2,1)S(1)}, u32[]{:S(2)}) copy-start(bf16[1280,3072]{1,0:T(8,128)(2,1)S(1)} %add_convert_fusion) | copy-start | bytes 23592964
  315.4 15.9 %slice-start.7 = ((s8[9437184]{0:T(1024)(128)(4,1)}), s8[4194304]{0:T(1024)(128)(4,1)S(1)}, s32[]{:S(2)}) async-start(s8[9437184]{0:T(1024)(128)(4,1)} %bitcast.289), calls=%async_computation.14 | async-start | bytes 8388608
  318.3 12.2 %copy-start.79 = (bf16[2,768,128]{2,1,0:T(8,128)(2,1)S(1)}, bf16[2,768,128]{2,1,0:T(8,128)(2,1)}, u32[]{:S(2)}) copy-start(bf16[2,768,128]{2,1,0:T(8,128)(2,1)} %param.49) | copy-start | bytes 1179652
  318.3 12.2 %copy-start.136 = (s32[1280]{0:T(1024)S(1)}, s32[1280]{0:T(1024)}, u32[]{:S(2)}) copy-start(s32[1280]{0:T(1024)} %eq.63) | copy-start | bytes 15364
  318.3 12.9 %slice-start.8 = ((s8[9437184]{0:T(1024)(128)(4,1)}), s8[4194304]{0:T(1024)(128)(4,1)S(1)}, s32[]{:S(2)}) async-start(s8[9437184]{0:T(1024)(128)(4,1)} %bitcast.289), calls=%async_computation.15 | async-start | bytes 8388608
  318.3 12.9 %slice-start.9 = ((s8[9437184]{0:T(1024)(128)(4,1)}), s8[1048576]{0:T(1024)(128)(4,1)S(1)}, s32[]{:S(2)}) async-start(s8[9437184]{0:T(1024)(128)(4,1)} %bitcast.289), calls=%async_computation.16 | async-start | bytes 2097152
  331.2 10.8 copy-start.54
  342.0 39.5 %copy-start.91 = (bf16[1280,128]{1,0:T(8,128)(2,1)}, bf16[1280,128]{1,0:T(8,128)(2,1)S(1)}, u32[]{:S(2)}) copy-start(bf16[1280,128]{1,0:T(8,128)(2,1)S(1)} %fusion.61) | copy-start | bytes 983044
  399.3 11.7 %copy-start.10 = (bf16[1280,3072]{1,0:T(8,128)(2,1)}, bf16[1280,3072]{1,0:T(8,128)(2,1)S(1)}, u32[]{:S(2)}) copy-start(bf16[1280,3072]{1,0:T(8,128)(2,1)S(1)} %add_convert_fusion.1) | copy-start | bytes 23592964
  399.3 11.7 %copy-start.142 = (bf16[2,128,3072]{2,1,0:T(8,128)(2,1)S(1)}, bf16[2,128,3072]{2,1,0:T(8,128)(2,1)}, u32[]{:S(2)}) copy-start(bf16[2,128,3072]{2,1,0:T(8,128)(2,1)} %param.50) | copy-start | bytes 4718596
  414.2 10.6 copy-start.138
  414.2 10.6 copy-start.143
  431.1 50.2 %all-to-all-start.4 = ((bf16[4,640,768]{2,1,0:T(8,128)(2,1)}), bf16[4,640,768]{2,1,0:T(8,128)(2,1)}, u32[]{:S(2)}, u32[]{:S(2)}) async-start(bf16[4,640,768]{2,1,0:T(8,128)(2,1)} %bitcast.268), calls=%async_computation.4 | async-start | bytes 7864320 | tf_op jit(solution)/shard_map/all_to_all | solution.py:292
  441.7 10.7 copy-start.50
  481.3 50.3 %all-to-all-start.2 = ((bf16[4,640,768]{2,1,0:T(8,128)(2,1)}), bf16[4,640,768]{2,1,0:T(8,128)(2,1)}, u32[]{:S(2)}, u32[]{:S(2)}) async-start(bf16[4,640,768]{2,1,0:T(8,128)(2,1)} %bitcast.265), calls=%async_computation.2 | async-start | bytes 7864320 | tf_op jit(solution)/shard_map/all_to_all | solution.py:277
  486.3 331.6 %all-reduce.8.cloned.1.call-start = ((), (), s32[]{:S(2)}) async-start(), calls=%async_computation.5 | async-start | bytes 7077888 | tf_op jit(solution)/shard_map/psum | solution.py:358
  486.7 11.8 %slice-start = ((s8[7864320]{0:T(1024)(128)(4,1)}), s8[4194304]{0:T(1024)(128)(4,1)S(1)}, s32[]{:S(2)}) async-start(s8[7864320]{0:T(1024)(128)(4,1)} %bitcast.261), calls=%async_computation.7 | async-start | bytes 8388608
  548.2 14.3 %copy-start.111 = (s32[788,2]{0,1:T(2,128)S(1)}, s32[788,2]{0,1:T(2,128)}, u32[]{:S(2)}) copy-start(s32[788,2]{0,1:T(2,128)} %param.30) | copy-start | bytes 18916
  548.2 14.4 %copy-start.75 = (f32[788,8]{0,1:T(8,128)S(1)}, f32[788,8]{0,1:T(8,128)}, u32[]{:S(2)}) copy-start(f32[788,8]{0,1:T(8,128)} %copy-done.74) | copy-start | bytes 75652
  548.2 14.4 %copy-start.115 = (f32[788]{0:T(1024)S(1)}, f32[788]{0:T(1024)}, u32[]{:S(2)}) copy-start(f32[788]{0:T(1024)} %copy-done.114) | copy-start | bytes 9460
  548.2 14.4 %copy-start.121 = (f32[788]{0:T(1024)S(1)}, f32[788]{0:T(1024)}, u32[]{:S(2)}) copy-start(f32[788]{0:T(1024)} %copy-done.120) | copy-start | bytes 9460
  548.2 14.4 %copy-start.135 = (s32[788]{0:T(1024)S(1)}, s32[788]{0:T(1024)}, u32[]{:S(2)}) copy-start(s32[788]{0:T(1024)} %copy-done.134) | copy-start | bytes 9460
  548.3 14.4 %copy-start.140 = (bf16[128,8]{0,1:T(8,128)(2,1)S(1)}, bf16[128,8]{0,1:T(8,128)(2,1)}, u32[]{:S(2)}) copy-start(bf16[128,8]{0,1:T(8,128)(2,1)} %param.47) | copy-start | bytes 6148
  563.0 12.6 %copy-start.68 = (bf16[788,128]{1,0:T(8,128)(2,1)}, bf16[788,128]{1,0:T(8,128)(2,1)S(1)}, u32[]{:S(2)}) copy-start(bf16[788,128]{1,0:T(8,128)(2,1)S(1)} %fusion.73) | copy-start | bytes 605188
  673.2 407.0 %all-reduce.10.cloned.1.call-start = ((), (), s32[]{:S(2)}) async-start(), calls=%async_computation.6 | async-start | bytes 15728640 | tf_op jit(solution)/shard_map/psum | solution.py:373
  689.6 41.5 %copy-start.71 = (bf16[788,128]{1,0:T(8,128)(2,1)S(1)}, bf16[788,128]{1,0:T(8,128)(2,1)}, u32[]{:S(2)}) copy-start(bf16[788,128]{1,0:T(8,128)(2,1)} %fusion.81) | copy-start | bytes 605188
  690.6 42.1 %copy-start.67 = (bf16[788,128]{1,0:T(8,128)(2,1)S(1)}, bf16[788,128]{1,0:T(8,128)(2,1)}, u32[]{:S(2)}) copy-start(bf16[788,128]{1,0:T(8,128)(2,1)} %fusion.80) | copy-start | bytes 605188
  817.8 269.7 %copy-start.88 = (f32[768,128]{1,0:T(8,128)S(1)}, f32[768,128]{1,0:T(8,128)}, u32[]{:S(2)}) copy-start(f32[768,128]{1,0:T(8,128)} %get-tuple-element.70) | copy-start | bytes 1179652
  817.9 270.5 %copy-start.87 = (f32[128,768]{1,0:T(8,128)S(1)}, f32[128,768]{1,0:T(8,128)}, u32[]{:S(2)}) copy-start(f32[128,768]{1,0:T(8,128)} %get-tuple-element.71) | copy-start | bytes 1179652
  817.9 271.2 %copy-start.86 = (f32[768,128]{1,0:T(8,128)S(1)}, f32[768,128]{1,0:T(8,128)}, u32[]{:S(2)}) copy-start(f32[768,128]{1,0:T(8,128)} %get-tuple-element.72) | copy-start | bytes 1179652
  817.9 271.9 %copy-start.85 = (f32[128,768]{1,0:T(8,128)S(1)}, f32[128,768]{1,0:T(8,128)}, u32[]{:S(2)}) copy-start(f32[128,768]{1,0:T(8,128)} %get-tuple-element.73) | copy-start | bytes 1179652
  1080.2 10.3 copy-start.84
  (117 other events, 445.9 us)
Sparse Core Ops, SparseCore 0:
  673.3 144.4 all-reduce.7
  823.5 256.7 all-reduce.9
where the time goes:
time: 1110 us; the launch traced here: 1100 us
  waiting for transfers between devices  430 us (39%)
  matrix products  333 us (30%)
  local copies, waits for them, and re-layouts  194 us (17%)
  other arithmetic  66.4 us (6%)
  blocking collectives  40.4 us (4%)
  starting transfers between devices  24.7 us (2%)
  between operations  16.1 us (1%)
    psum x1, waiting for transfers between devices, body(): lax.psum((up_a_grad, up_b_grad, down_a_grad, down_b_grad), 'dp')  262 us
    dot_general x27, matrix products, product(): return jnp.dot(first_op, second_op, preferred_element_type=jnp.float32)  153 us
    dot_general x27, matrix products, product_nt(): lax.dot_general(first_op, second_op, (((1,), (1,)), ((), ())), preferred_...  114 us
    psum x1, waiting for transfers between devices, body(): lax.psum((query_a_grad, query_b_grad, key_a_grad, key_b_grad, value_a_gra...  73.4 us
    all_to_all x1, waiting for transfers between devices, body(): lax.all_to_all(send_grads, 'expert', split_axis=0, concat_axis=0, tiled=T...  40.7 us
    psum x1, blocking collectives, body(): lax.psum((query_a_grad, query_b_grad, key_a_grad, key_b_grad, value_a_gra...  40.4 us
    reshape x8, local copies, waits for them, and re-layouts, head_split(): return row_block.reshape(-1, SEQ, HEADS, HEAD_DIM)  39.2 us
    dot_general x18, matrix products, product_tn(): lax.dot_general(first_op, second_op, (((0,), (0,)), ((), ())), preferred_...  38.3 us
  transfers between devices with their start and end apart: 7, of which 6 were waited for; matrix products, arithmetic and copies ran while one was open for 17% of the time, Pallas kernels for 0%

commit v1 on v0

v1 whole, which is shorter than its diff:
```python
import functools
import math

import jax
import jax.numpy as jnp
from jax import lax
from jax.experimental import pallas as pl
from jax.experimental.pallas import tpu as pltpu
from jax.sharding import PartitionSpec as P

HEAD_DIM = 64
RANK = 16
SEQ = 197
EPS = 1e-06
BF = jnp.bfloat16
F32 = jnp.float32
I32 = jnp.int32
LOG2E = math.log2(math.e)
SCALE2 = HEAD_DIM ** (-0.5) * LOG2E
NEG = -1e30
TILE = 256
CHUNK = 768
VMEM = pl.BlockSpec(memory_space=pltpu.VMEM)
SMEM = pl.BlockSpec(memory_space=pltpu.SMEM)


def up16(n):
    return -(-n // 16) * 16


def nn(a, b):
    return jnp.dot(a, b, preferred_element_type=F32)


def nt(a, b):
    return lax.dot_general(a, b, (((1,), (1,)), ((), ())), preferred_element_type=F32)


def tn(a, b):
    return lax.dot_general(a, b, (((0,), (0,)), ((), ())), preferred_element_type=F32)


def params(mib):
    return pltpu.CompilerParams(vmem_limit_bytes=mib * 1024 * 1024)


def image_banks(banks, row, images):
    bank = jnp.full(row.shape, banks[0], I32)
    for i in range(1, images):
        bank = jnp.where(row >= SEQ * i, banks[i], bank)
    return bank


def bank_mask(banks, start, count, images, width):
    row = lax.broadcasted_iota(I32, (count, width), 0) + start
    col = lax.broadcasted_iota(I32, (count, width), 1)
    return (col // RANK == image_banks(banks, row, images)).astype(F32)


def norm_parts(x):
    mean = jnp.mean(x, axis=-1, keepdims=True)
    cen = x - mean
    rstd = lax.rsqrt(jnp.mean(cen * cen, axis=-1, keepdims=True) + EPS)
    return cen * rstd, rstd


def norm_back(xhat, rstd, gain, grad):
    gy = grad * gain
    return rstd * (
        gy
        - jnp.mean(gy, axis=-1, keepdims=True)
        - xhat * jnp.mean(gy * xhat, axis=-1, keepdims=True)
    )


def attn_fwd_kernel(
    banks, tok, g1, g2, wq, wk, wv, wo, aq, bq, ak, bk, av, bv, ao, bo, rwt, ra, rbt,
    n1_o, q_o, k_o, v_o, lq_o, lk_o, lv_o, att_o, lo_o, mid_o, n2_o, lr_o, pt_o, lse_o,
    tokp, lset,
):
    rows = tok.shape[0]
    rp = n1_o.shape[0]
    images = rows // SEQ
    d = tok.shape[1]
    width = aq.shape[1]
    win = lse_o.shape[2]
    step_rows = 16 * (SEQ // 16)
    tokp[pl.ds(rp - 16, 16), :] = jnp.zeros((16, d), BF)
    tokp[0:rows, :] = tok[...]

    def ln1(i, _):
        r = pl.multiple_of(i * 32, 32)
        xhat, _r = norm_parts(tokp[pl.ds(r, 32), :].astype(F32))
        n1_o[pl.ds(r, 32), :] = (g1[...] * xhat).astype(BF)
        return 0

    lax.fori_loop(0, rp // 32, ln1, 0)
    half = rp // 2

    def qkv(i, _):
        r = pl.multiple_of(i * half, 16)
        x = n1_o[pl.ds(r, half), :]
        mask = bank_mask(banks, r, half, images, width)
        for w, a, b, out, low in (
            (wq, aq, bq, q_o, lq_o),
            (wk, ak, bk, k_o, lk_o),
            (wv, av, bv, v_o, lv_o),
        ):
            u = (nn(x, a[...]) * mask).astype(BF)
            low[pl.ds(r, half), :] = u
            out[pl.ds(r, half), :] = (nn(x, w[...]) + nn(u, b[...])).astype(BF)
        return 0

    lax.fori_loop(0, 2, qkv, 0)

    lane = lax.broadcasted_iota(I32, (win, 128), 1)
    first = lane < HEAD_DIM
    row_i = lax.broadcasted_iota(I32, (win, 128), 0)
    keys_i = lax.broadcasted_iota(I32, (win, win), 1)

    def image(i, _):
        off = pl.multiple_of(i * step_rows, 64)
        lo = i * (SEQ - step_rows)
        bias = jnp.where((keys_i >= lo) & (keys_i < lo + SEQ), 0.0, NEG)
        keep = row_i < lo
        lset[...] = jnp.zeros_like(lset)
        lse_tile = jnp.zeros((win, 128), F32)
        for p in range(d // 128):
            cols = slice(p * 128, p * 128 + 128)
            qp = q_o[pl.ds(off, win), cols]
            kp = k_o[pl.ds(off, win), cols]
            vp = v_o[pl.ds(off, win), cols]
            outs = []
            for h in range(2):
                mine = first if h == 0 else jnp.logical_not(first)
                qm = jnp.where(mine, qp, jnp.zeros_like(qp))
                s = nt(qm, kp) * SCALE2 + bias
                top = jnp.max(s, axis=-1, keepdims=True)
                e = jnp.exp2(s - top)
                den = jnp.sum(e, axis=-1, keepdims=True)
                w = (e * pl.reciprocal(den)).astype(BF)
                outs.append(nn(w, vp))
                lse = top + jnp.log2(den)
                lse_tile = jnp.where(lane == 2 * p + h, lse, lse_tile)
            new = jnp.where(first, outs[0], outs[1]).astype(BF)
            att_o[pl.ds(off, win), cols] = jnp.where(keep, att_o[pl.ds(off, win), cols], new)
        lset[0:win, :] = lse_tile
        lse_o[i] = jnp.transpose(lset[...])[0 : lse_o.shape[1], 0:win]
        return 0

    lax.fori_loop(0, images, image, 0)

    def out_proj(i, _):
        r = pl.multiple_of(i * half, 16)
        x = att_o[pl.ds(r, half), :]
        mask = bank_mask(banks, r, half, images, width)
        u = (nn(x, ao[...]) * mask).astype(BF)
        lo_o[pl.ds(r, half), :] = u
        mid_o[pl.ds(r, half), :] = (
            tokp[pl.ds(r, half), :].astype(F32) + nn(x, wo[...]) + nn(u, bo[...])
        )
        return 0

    lax.fori_loop(0, 2, out_proj, 0)

    def ln2(i, _):
        r = pl.multiple_of(i * 32, 32)
        xhat, _r = norm_parts(mid_o[pl.ds(r, 32), :])
        n2_o[pl.ds(r, 32), :] = (g2[...] * xhat).astype(BF)
        return 0

    lax.fori_loop(0, rp // 32, ln2, 0)
    x = n2_o[...]
    u = (nn(x, ra[...]) * bank_mask(banks, 0, rp, images, width)).astype(BF)
    lr_o[...] = u
    logits = nt(rwt[...], x) + nt(rbt[...], u)
    e = jnp.exp(logits - jnp.max(logits, axis=0, keepdims=True))
    pt_o[...] = e / jnp.sum(e, axis=0, keepdims=True)


def attn_forward(banks, tok, g1, g2, ws):
    rows, d = tok.shape
    rp = 32 * (-(-rows // 32))
    images = rows // SEQ
    step_rows = 16 * (SEQ // 16)
    win = rp - step_rows * (images - 1)
    width = ws[4].shape[1]
    experts = ws[12].shape[0]
    heads_pad = 16 * (-(-d // (16 * HEAD_DIM)))
    bfd = jax.ShapeDtypeStruct((rp, d), BF)
    low = jax.ShapeDtypeStruct((rp, width), BF)
    out_shape = (
        bfd, bfd, bfd, bfd, low, low, low, bfd, low,
        jax.ShapeDtypeStruct((rp, d), F32), bfd, low,
        jax.ShapeDtypeStruct((experts, rp), F32),
        jax.ShapeDtypeStruct((images, heads_pad, win), F32),
    )
    return pl.pallas_call(
        attn_fwd_kernel,
        out_shape=out_shape,
        in_specs=[SMEM] + [VMEM] * 18,
        out_specs=tuple([VMEM] * len(out_shape)),
        scratch_shapes=[pltpu.VMEM((rp, d), BF), pltpu.VMEM((256, 128), F32)],
        compiler_params=params(56),
        name="attn_fwd",
    )(banks, tok, g1, g2, *ws)


def tables_kernel(eidx, routes, posr_o, posc_o):
    groups, _, rp = routes.shape
    local = posr_o.shape[0] // groups
    row = lax.broadcasted_iota(I32, (rp, rp), 0)
    col = lax.broadcasted_iota(I32, (rp, rp), 1)
    upper = (row < col).astype(BF)
    upper_inc = (row <= col).astype(BF)
    lower = (col < row).astype(BF)
    lower_inc = (col <= row).astype(BF)
    which = lax.broadcasted_iota(I32, (groups * local, rp), 0)
    hot = jnp.zeros((groups * local, rp), F32)
    for s in range(groups):
        r0 = routes[s, 0:1, :]
        r1 = routes[s, 1:2, :]
        for j in range(local):
            e = eidx[0] * local + j
            hit = ((r0 == e) | (r1 == e)).astype(F32)
            hot = jnp.where(which == s * local + j, hit, hot)
    hb = hot.astype(BF)
    before = nn(hb, upper)
    with_own = nn(hb, upper_inc)
    posr_o[...] = jnp.where(with_own > before, before, -1.0)
    before = nt(lower, hb)
    with_own = nt(lower_inc, hb)
    posc_o[...] = jnp.where(with_own > before, before, -1.0)


def routing_tables(eidx, routes, local):
    groups, _, rp = routes.shape
    n = groups * local
    return pl.pallas_call(
        tables_kernel,
        out_shape=(jax.ShapeDtypeStruct((n, rp), F32), jax.ShapeDtypeStruct((rp, n), F32)),
        in_specs=[SMEM, VMEM],
        out_specs=(VMEM, VMEM),
        compiler_params=params(32),
        name="routing_tables",
    )(eidx, routes)


def gelu_parts(x):
    e = jnp.exp2((-0.5 * LOG2E) * (x * x))
    t = pl.reciprocal(1.0 + (0.3275911 / math.sqrt(2.0)) * jnp.abs(x))
    poly = 1.061405429 * 0.5
    for c in (-1.453152027, 1.421413741, -0.284496736, 0.254829592):
        poly = poly * t + 0.5 * c
    q = poly * t * e
    phi = jnp.where(x >= 0.0, 1.0 - q, q)
    return x * phi, phi + x * (e * (1.0 / math.sqrt(2.0 * math.pi)))


def expert_kernel(cfg, *refs):
    j, sources, combine, has_acc, cap, local, images = cfg
    refs = list(refs)
    take = lambda n: [refs.pop(0) for _ in range(n)]
    eidx, banks = take(2)
    posr, posc = take(2)
    gates = take(len(sources))
    nrows = take(len(sources))
    crows = take(len(sources))
    upw, upa, upb, dnw, dna, dnb = take(6)
    if combine:
        ret_in, grow_in, gg_in = take(3)
    if has_acc:
        acc_in = take(4)
    acc_out = take(4)
    if combine:
        grow_out = take(len(sources))
        mix_out = take(len(sources))
        gg_out = take(len(sources))
        xbuf, cbuf, gate_b, mask_b, gg_b, hid, dgl, stage, ret_b, grow_b = take(10)
    else:
        ret_b, grow_b, gg_rows = take(3)
        xbuf, cbuf, gate_b, mask_b, gg_b, hid, dgl = take(7)
    rp, d = nrows[0].shape
    ff = upw.shape[2]
    width = upa.shape[2]
    uaacc, ubacc, daacc, dbacc = acc_out
    if has_acc:
        for a, b in zip(acc_out, acc_in):
            a[...] = b[...]
    else:
        for a in acc_out:
            a[...] = jnp.zeros_like(a)
    slot_r = lax.broadcasted_iota(I32, (cap, rp), 0).astype(F32)
    slot_c = lax.broadcasted_iota(I32, (rp, cap), 1).astype(F32)
    token = lax.broadcasted_iota(I32, (1, rp), 1)
    experts = gates[0].shape[0]
    expert_row = lax.broadcasted_iota(I32, (experts, rp), 0)
    mine = expert_row == eidx[0] * local + j
    col_bank = (lax.broadcasted_iota(I32, (cap, width), 1) // RANK).astype(F32)

    def count_of(s, e):
        line = posr[s * local + e : s * local + e + 1, :]
        n = jnp.sum((line >= 0.0).astype(F32)).astype(I32)
        return ((n + 15) // 16) * 16

    offs = []
    off = jnp.int32(0)
    for i, s in enumerate(sources):
        off = pl.multiple_of(off, 16)
        offs.append(off)
        line = posr[s * local + j : s * local + j + 1, :]
        hit = line == slot_r
        gate_line = jnp.sum(jnp.where(mine, gates[i][...], 0.0), axis=0, keepdims=True)
        bank = jnp.full((1, rp), banks[s, 0], I32)
        for k in range(1, images):
            bank = jnp.where(token >= SEQ * k, banks[s, k], bank)
        gate = jnp.sum(jnp.where(hit, gate_line, 0.0), axis=1, keepdims=True)
        slot_bank = jnp.sum(jnp.where(hit, bank.astype(F32), 0.0), axis=1, keepdims=True)
        pick = hit.astype(F32).astype(BF)
        xbuf[pl.ds(off, cap), :] = nn(pick, nrows[i][...]).astype(BF)
        cbuf[pl.ds(off, cap), :] = nn(pick, crows[i][...]).astype(BF)
        gate_b[pl.ds(off, cap), :] = jnp.broadcast_to(gate, (cap, 128))
        mask_b[pl.ds(off, cap), :] = (col_bank == slot_bank).astype(F32)
        off = off + count_of(s, j)
    total = off
    last = pl.multiple_of(offs[-1] + cap, 16)
    xbuf[pl.ds(last, TILE), :] = jnp.zeros((TILE, d), BF)
    cbuf[pl.ds(last, TILE), :] = jnp.zeros((TILE, d), BF)
    gate_b[pl.ds(last, TILE), :] = jnp.zeros((TILE, 128), F32)
    mask_b[pl.ds(last, TILE), :] = jnp.zeros((TILE, width), F32)
    tiles = (total + TILE - 1) // TILE
    nc = ff // CHUNK

    def tile(t, _):
        rs = pl.ds(pl.multiple_of(t * TILE, TILE), TILE)
        x = xbuf[rs, :]
        m = mask_b[rs, :]
        u = (nn(x, upa[0]) * m).astype(BF)
        out = jnp.zeros((TILE, d), F32)
        ud = jnp.zeros((TILE, width), F32)
        for c in range(nc):
            cs = slice(c * CHUNK, (c + 1) * CHUNK)
            h, dg = gelu_parts(nn(x, upw[0, :, cs]) + nn(u, upb[0, :, cs]))
            hb = h.astype(BF)
            hid[:, cs] = hb
            dgl[:, cs] = dg
            ud = ud + nn(hb, dna[0, cs, :])
            out = out + nn(hb, dnw[0, cs, :])
        udl = (ud * m).astype(BF)
        ret = (out + nn(udl, dnb[0])).astype(BF).astype(F32)
        cot = cbuf[rs, :].astype(F32)
        gate = gate_b[rs, 0:1]
        gg_b[rs, :] = jnp.broadcast_to(jnp.sum(cot * ret, axis=1, keepdims=True), (TILE, 128))
        ret_b[rs, :] = (gate * ret).astype(BF)
        g = (gate * cot).astype(BF)
        gud = (nt(g, dnb[0]) * m).astype(BF)
        dbacc[...] += tn(udl, g)
        gul = jnp.zeros((TILE, width), F32)
        gr = jnp.zeros((TILE, d), F32)
        for c in range(nc):
            cs = slice(c * CHUNK, (c + 1) * CHUNK)
            gh = nt(g, dnw[0, cs, :]) + nt(gud, dna[0, cs, :])
            gp = (gh * dgl[:, cs]).astype(BF)
            gul = gul + nt(gp, upb[0, :, cs])
            gr = gr + nt(gp, upw[0, :, cs])
            ubacc[:, cs] += tn(u, gp)
            daacc[:, cs] += tn(gud, hid[:, cs])
        guu = (gul * m).astype(BF)
        uaacc[...] += tn(guu, x)
        grow_b[rs, :] = (gr + nt(guu, upa[0])).astype(BF)
        return 0

    lax.fori_loop(0, tiles, tile, 0)
    done = pl.multiple_of(tiles * TILE, 16)
    ret_b[pl.ds(done, cap), :] = jnp.zeros((cap, d), BF)
    grow_b[pl.ds(done, cap), :] = jnp.zeros((cap, d), BF)
    gg_b[pl.ds(done, cap), :] = jnp.zeros((cap, 128), F32)
    gg_lines = []
    for i, s in enumerate(sources):
        line = posr[s * local + j : s * local + j + 1, :]
        col = gg_b[pl.ds(offs[i], cap), 0:1]
        gg_lines.append(
            jnp.sum(jnp.where(line == slot_r, col, 0.0), axis=0, keepdims=True)
        )
    if not combine:
        for i, s in enumerate(sources):
            gg_rows[s : s + 1, :] = gg_lines[i]
        return
    base = jnp.int32(0)
    firsts = {}
    for s in range(len(banks_range(posr, local))):
        firsts[s] = pl.multiple_of(base, 16)
        base = base + count_of(s, 0)
    for i, s in enumerate(sources):
        p0 = (posc[:, s * local : s * local + 1] == slot_c).astype(F32).astype(BF)
        p1 = (posc[:, s * local + 1 : s * local + 2] == slot_c).astype(F32).astype(BF)
        for mine_b, other, result in (
            (grow_b, grow_in, grow_out[i]),
            (ret_b, ret_in, mix_out[i]),
        ):
            result[...] = (
                nn(p0, other[pl.ds(firsts[s], cap), :]) + nn(p1, mine_b[pl.ds(offs[i], cap), :])
            ).astype(BF)
        e0 = eidx[0] * local
        gg_out[i][...] = jnp.where(
            expert_row == e0,
            gg_in[s : s + 1, :],
            jnp.where(expert_row == e0 + 1, gg_lines[i], 0.0),
        )


def banks_range(posr, local):
    return range(posr.shape[0] // local)


def expert_call(j, sources, combine, eidx, banks, tables, gates, nrows, crows, ws, cap, first, acc):
    posr, posc = tables
    rp, d = nrows[0].shape
    images = banks.shape[1]
    upw, upa, upb, dnw, dna, dnb = ws
    local, _, ff = upw.shape
    width = upa.shape[2]
    experts = gates[0].shape[0]
    n = len(sources)
    cfg = (j, tuple(sources), combine, acc is not None, cap, local, images)
    buf_rows = n * cap + TILE + cap
    args = [eidx, banks, posr, posc]
    args += [gates[s] for s in sources] + [nrows[s] for s in sources] + [crows[s] for s in sources]
    in_specs = [SMEM, SMEM] + [VMEM] * (2 + 3 * n)
    args += list(ws)
    for w in ws:
        in_specs.append(pl.BlockSpec((1,) + w.shape[1:], lambda i: (j, 0, 0)))
    whole = lambda shape: pl.BlockSpec(shape, lambda i: (0,) * len(shape))
    in_specs = [
        s if s.memory_space == pltpu.SMEM or s.block_shape is not None else s for s in in_specs
    ]
    if combine:
        args += list(first)
        in_specs += [VMEM] * 3
    if acc is not None:
        args += list(acc)
        in_specs += [VMEM] * 4
    acc_shapes = ((width, d), (width, ff), (width, ff), (width, d))
    out_shape = [jax.ShapeDtypeStruct(s, F32) for s in acc_shapes]
    if combine:
        out_shape += [jax.ShapeDtypeStruct((rp, d), BF)] * (2 * n)
        out_shape += [jax.ShapeDtypeStruct((experts, rp), F32)] * n
    else:
        out_shape += [jax.ShapeDtypeStruct((buf_rows, d), BF)] * 2
        out_shape += [jax.ShapeDtypeStruct((n, rp), F32)]
    scratch = [
        pltpu.VMEM((buf_rows, d), BF),
        pltpu.VMEM((buf_rows, d), BF),
        pltpu.VMEM((buf_rows, 128), F32),
        pltpu.VMEM((buf_rows, width), F32),
        pltpu.VMEM((buf_rows, 128), F32),
        pltpu.VMEM((TILE, ff), BF),
        pltpu.VMEM((TILE, ff), F32),
    ]
    if combine:
        scratch += [
            pltpu.VMEM((16, 128), BF),
            pltpu.VMEM((buf_rows, d), BF),
            pltpu.VMEM((buf_rows, d), BF),
        ]
    return pl.pallas_call(
        functools.partial(expert_kernel, cfg),
        grid=(1,),
        out_shape=tuple(out_shape),
        in_specs=in_specs,
        out_specs=tuple([VMEM] * len(out_shape)),
        scratch_shapes=scratch,
        compiler_params=params(60),
        name="experts",
    )(*args)


def attn_bwd_kernel(
    banks, tok, cot, g1, g2, wq, wk, wv, wo, aq, bq, ak, bk, av, bv, ao, bo, rwt, ra, rbt,
    n1, q, k, v, lq, lk, lv, att, lo, mid, n2, lr, pt, lse, gpt, p0, p1, p2,
    inp_o, gr_o, rb_o,
    gmid, gml, ga, gq, gk, gv,
):
    rows, d = tok.shape
    rp = n1.shape[0]
    images = rows // SEQ
    width = aq.shape[1]
    win = lse.shape[2]
    step_rows = 16 * (SEQ // 16)
    probs = pt[...]
    gp = gpt[...]
    glt = (probs * (gp - jnp.sum(gp * probs, axis=0, keepdims=True))).astype(BF)
    rb_o[...] = nn(glt, lr[...])
    mask = bank_mask(banks, 0, rp, images, width)
    gu = (tn(glt, rbt[...]) * mask).astype(BF)
    gr_o[8] = tn(gu, n2[...])
    gmid[...] = tn(glt, rwt[...]) + nt(gu, ra[...])

    def ln2(i, _):
        rs = pl.ds(pl.multiple_of(i * 32, 32), 32)
        grad = gmid[rs, :] + (p0[rs, :].astype(F32) + p1[rs, :].astype(F32) + p2[rs, :].astype(F32))
        xhat, rstd = norm_parts(mid[rs, :])
        g = cot[rs, :].astype(F32) + norm_back(xhat, rstd, g2[...], grad)
        gmid[rs, :] = g
        gml[rs, :] = g.astype(BF)
        return 0

    lax.fori_loop(0, rp // 32, ln2, 0)
    g = gml[...]
    gr_o[7] = tn(lo[...], g)
    gu = (nt(g, bo[...]) * mask).astype(BF)
    gr_o[6] = tn(gu, att[...])
    ga[...] = (nt(g, wo[...]) + nt(gu, ao[...])).astype(BF)

    lane = lax.broadcasted_iota(I32, (win, 128), 1)
    first = lane < HEAD_DIM
    row_i = lax.broadcasted_iota(I32, (win, 128), 0)
    key_i = lax.broadcasted_iota(I32, (win, win), 0)
    query_i = lax.broadcasted_iota(I32, (win, win), 1)

    def image(i, _):
        off = pl.multiple_of(i * step_rows, 64)
        start = i * (SEQ - step_rows)
        bias = jnp.where(
            (key_i >= start) & (key_i < start + SEQ) & (query_i >= start) & (query_i < start + SEQ),
            0.0,
            NEG,
        )
        keep = row_i < start
        ws = pl.ds(off, win)
        for p in range(d // 128):
            cols = slice(p * 128, p * 128 + 128)
            qp = q[ws, cols]
            kp = k[ws, cols]
            vp = v[ws, cols]
            gap = ga[ws, cols]
            rq, rk, rv = [], [], []
            for h in range(2):
                mine = first if h == 0 else jnp.logical_not(first)
                km = jnp.where(mine, kp, jnp.zeros_like(kp))
                vm = jnp.where(mine, vp, jnp.zeros_like(vp))
                prob = jnp.exp2(
                    nt(km, qp) * SCALE2 + bias - lse[i, 2 * p + h : 2 * p + h + 1, :]
                )
                gw = nt(vm, gap)
                delta = jnp.sum(gw * prob, axis=0, keepdims=True)
                gs = (prob * (gw - delta)).astype(BF)
                rv.append(nn(prob.astype(BF), gap))
                rk.append(nn(gs, qp))
                rq.append(tn(gs, kp))
            for parts, ref, scale in ((rq, gq, 0.125), (rk, gk, 0.125), (rv, gv, 1.0)):
                new = (jnp.where(first, parts[0], parts[1]) * scale).astype(BF)
                ref[ws, cols] = jnp.where(keep, ref[ws, cols], new)
        return 0

    lax.fori_loop(0, images, image, 0)
    x = n1[...]
    total = None
    for n, (grad, low, w, a, b) in enumerate(
        ((gq, lq, wq, aq, bq), (gk, lk, wk, ak, bk), (gv, lv, wv, av, bv))
    ):
        g = grad[...]
        gr_o[2 * n + 1] = tn(low[...], g)
        gu = (nt(g, b[...]) * mask).astype(BF)
        gr_o[2 * n] = tn(gu, x)
        part = nt(g, w[...]) + nt(gu, a[...])
        total = part if total is None else total + part

    whole = rows // 16 * 16
    for r, count in [(s, min(112, whole - s)) for s in range(0, whole, 112)] + (
        [(whole, rows - whole)] if rows > whole else []
    ):
        rs = slice(r, r + count)
        xhat, rstd = norm_parts(tok[rs, :].astype(F32))
        inp_o[rs, :] = gmid[rs, :] + norm_back(xhat, rstd, g1[...], total[rs, :])


def attn_backward(banks, tok, cot, g1, g2, ws, kept, gpt, parts):
    rows, d = tok.shape
    rp = cot.shape[0]
    width = ws[4].shape[1]
    experts = gpt.shape[0]
    bfd = pltpu.VMEM((rp, d), BF)
    out_shape = (
        jax.ShapeDtypeStruct((rows, d), F32),
        jax.ShapeDtypeStruct((9, width, d), F32),
        jax.ShapeDtypeStruct((experts, width), F32),
    )
    return pl.pallas_call(
        attn_bwd_kernel,
        out_shape=out_shape,
        in_specs=[SMEM] + [VMEM] * 37,
        out_specs=(VMEM,) * 3,
        scratch_shapes=[pltpu.VMEM((rp, d), F32), bfd, bfd, bfd, bfd, bfd],
        compiler_params=params(60),
        name="attn_bwd",
    )(banks, tok, cot, g1, g2, *ws, *kept, gpt, *parts)


def hop(x, axis, k):
    n = lax.axis_size(axis)
    return lax.ppermute(x, axis, [(i, i ^ k) for i in range(n)])


def bits(axis):
    n = lax.axis_size(axis)
    return [1 << i for i in range(n.bit_length() - 1)]


def all_reduce(buf, steps):
    trail = []
    for axis, k in steps:
        half = buf.shape[0] // 2
        bit = (lax.axis_index(axis) // k) % 2
        keep = lax.dynamic_slice_in_dim(buf, bit * half, half, 0)
        send = lax.dynamic_slice_in_dim(buf, (1 - bit) * half, half, 0).astype(BF)
        buf = keep + hop(send, axis, k).astype(F32)
        trail.append((axis, k, bit))
    buf = buf.astype(BF)
    for axis, k, bit in reversed(trail):
        other = hop(buf, axis, k)
        buf = jnp.where(
            bit == 0,
            jnp.concatenate([buf, other], axis=0),
            jnp.concatenate([other, buf], axis=0),
        )
    return buf.astype(F32)


def gather4(x):
    near = hop(x, "expert", 1)
    far = hop(x, "expert", 2)
    return [x, near, far, hop(far, "expert", 1)]


def body(
    tokens, cotangent, bank_ids, routes, attn_gain, expert_gain, query_w, key_w, value_w, out_w,
    query_a, query_b, key_a, key_b, value_a, value_b, out_a, out_b, router_w, router_a, router_b,
    up_w, up_a, up_b, down_w, down_a, down_b,
):
    rows, d = tokens.shape
    rp = 32 * (-(-rows // 32))
    width = query_a.shape[1]
    local = up_w.shape[0]
    groups = lax.axis_size("expert")
    experts = local * groups
    cap = 13 * rows // (4 * experts)
    me = lax.axis_index("expert").astype(I32).reshape(1)
    cot = jnp.pad(cotangent, ((0, rp - rows), (0, 0)))
    crows = gather4(cot)
    routes_t = jnp.pad(routes.T, ((0, 0), (0, rp - rows)), constant_values=-1)
    routes_all = jnp.stack(gather4(routes_t))
    banks_all = jnp.stack(gather4(bank_ids))
    tables = routing_tables(me, routes_all, local)
    g1 = attn_gain.reshape(1, d)
    g2 = expert_gain.reshape(1, d)
    ws = (
        query_w, key_w, value_w, out_w, query_a, query_b, key_a, key_b, value_a, value_b,
        out_a, out_b, router_w.T, router_a, router_b.T,
    )
    kept = attn_forward(bank_ids, tokens, g1, g2, ws)
    mid, n2, pt = kept[9], kept[10], kept[12]
    nrows = gather4(n2)
    gates = gather4(pt)
    ews = (up_w, up_a, up_b, down_w, down_a, down_b)
    common = (me, banks_all, tables, gates, nrows, crows, ews, cap)
    e0 = expert_call(0, (0, 1, 2, 3), False, *common, None, None)
    acc0, first = e0[:4], e0[4:]
    far = expert_call(1, (2, 3), True, *common, first, None)
    acc1 = far[:4]
    near = expert_call(1, (0, 1), True, *common, first, acc1)
    acc1 = near[:4]

    def fold(a, b):
        mine = a.astype(F32) + hop(b, "expert", 1).astype(F32)
        return hop(mine.astype(a.dtype), "expert", 2)

    grow_far = fold(far[4], far[5])
    gg_far = fold(far[8], far[9])
    mix_far = fold(far[6], far[7])
    grow_near = hop(near[5], "expert", 1)
    gg_near = hop(near[9], "expert", 1)
    mix_near = hop(near[7], "expert", 1)
    gpt = near[8] + gg_near + gg_far
    mixed = mid[:rows] + (
        near[6][:rows].astype(F32) + mix_near[:rows].astype(F32) + mix_far[:rows].astype(F32)
    )
    input_grad, grads, rb = attn_backward(
        bank_ids, tokens, cot, g1, g2, ws, kept, gpt, (near[4], grow_near, grow_far)
    )
    dp_steps = [("dp", k) for k in bits("dp")]
    ex_steps = [("expert", k) for k in bits("expert")]
    pad = jnp.zeros((experts, d - width), F32)
    flat = jnp.concatenate([grads.reshape(9 * width, d), jnp.concatenate([rb, pad], axis=1)])
    shares = lax.axis_size("dp") * groups
    extra = -flat.shape[0] % shares
    flat = jnp.pad(flat, ((0, extra), (0, 0)))
    flat = all_reduce(flat, ex_steps + dp_steps)
    parts = [flat[i * width : (i + 1) * width] for i in range(9)]
    rb = flat[9 * width : 9 * width + experts, :width].T
    outs = []
    for acc in (acc0, acc1):
        outs.append(all_reduce(jnp.concatenate(acc, axis=1), dp_steps))
    ff = up_w.shape[2]
    both = jnp.stack(outs)
    ua = jnp.swapaxes(both[:, :, :d], 1, 2)
    ub = both[:, :, d : d + ff]
    da = jnp.swapaxes(both[:, :, d + ff : d + 2 * ff], 1, 2)
    db = both[:, :, d + 2 * ff :]
    return (
        mixed.astype(BF), input_grad,
        parts[0].T, parts[1], parts[2].T, parts[3], parts[4].T, parts[5], parts[6].T, parts[7],
        parts[8].T, rb, ua, ub, da, db,
    )


def solution(mesh):
    split = P(("dp", "expert"), None)
    by_expert = P("expert", None, None)
    in_specs = (split, split, P(("dp", "expert")), split) + (P(),) * 17 + (by_expert,) * 6
    out_specs = (split, split) + (P(),) * 10 + (by_expert,) * 4
    return jax.shard_map(body, mesh=mesh, in_specs=in_specs, out_specs=out_specs, check_vma=False)
```

time: 1110 us -> 515 us (0.46); the launches traced: 1100 us -> 523 us
  matrix products: 333 us -> 0 us
  waiting for transfers between devices: 430 us -> 162 us
  Pallas kernels: 0 us -> 198 us
  local copies, waits for them, and re-layouts: 194 us -> 30.2 us
  starting transfers between devices: 24.7 us -> 112 us
  other arithmetic: 66.4 us -> 18.1 us
  blocking collectives: 40.4 us -> 0 us
  between operations: 16.1 us -> 1.52 us
    psum x2 -> x0, waiting for transfers between devices: 336 us -> none  [the longest x1 262 us: body(): lax.psum((up_a_grad, up_b_grad, down_a_grad, down_b_grad), 'dp')]
    dot_general x78 -> x0, matrix products: 333 us -> none  [the longest x27 153 us: product(): return jnp.dot(first_op, second_op, preferred_element_type=jnp.float32)]
    pallas_call x0 -> x6, Pallas kernels: none -> 198 us  [the longest x3 120 us: expert_call(): pl.pallas_call(functools.partial(expert_kernel, cfg), grid=(1,), out_shap...]
    ppermute x0 -> x46, waiting for transfers between devices: none -> 162 us  [hop(): return lax.ppermute(x, axis, [(i, i ^ k) for i in range(n)])]
    ppermute x0 -> x46, starting transfers between devices: none -> 112 us  [hop(): return lax.ppermute(x, axis, [(i, i ^ k) for i in range(n)])]
    all_to_all x5 -> x0, waiting for transfers between devices: 93.8 us -> none  [the longest x1 40.7 us: body(): lax.all_to_all(send_grads, 'expert', split_axis=0, concat_axis=0, tiled=T...]
    gather x5 -> x0, local copies, waits for them, and re-layouts: 50.5 us -> none  [the longest x1 12.3 us: body(): padded_grads[route_index]]
    psum x1 -> x0, blocking collectives: 40.4 us -> none  [body(): lax.psum((query_a_grad, query_b_grad, key_a_grad, key_b_grad, value_a_gra...]
  transfers between devices with their start and end apart: 7 -> 46, of which waited for: 6 -> 24; matrix products, arithmetic and copies ran while one was open for 17% -> 5% of each run, Pallas kernels for 0% -> 23%
where the time goes in v1:
time: 515 us; the launch traced here: 523 us
  Pallas kernels  198 us (38%)
  waiting for transfers between devices  162 us (31%)
  starting transfers between devices  112 us (22%)
  local copies, waits for them, and re-layouts  30.2 us (6%)
  other arithmetic  18.1 us (4%)
    ppermute x46, waiting for transfers between devices, hop(): return lax.ppermute(x, axis, [(i, i ^ k) for i in range(n)])  162 us
    pallas_call x3, Pallas kernels, expert_call(): pl.pallas_call(functools.partial(expert_kernel, cfg), grid=(1,), out_shap...  120 us
    ppermute x46, starting transfers between devices, hop(): return lax.ppermute(x, axis, [(i, i ^ k) for i in range(n)])  112 us
    pallas_call x1, Pallas kernels, attn_backward(): pl.pallas_call(attn_bwd_kernel, out_shape=out_shape, in_specs=[SMEM] + [V...  45.1 us
    pallas_call x1, Pallas kernels, attn_forward(): pl.pallas_call(attn_fwd_kernel, out_shape=out_shape, in_specs=[SMEM] + [V...  31.9 us
    unnamed x69, local copies, waits for them, and re-layouts  20.6 us
  transfers between devices with their start and end apart: 46, of which 24 were waited for; matrix products, arithmetic and copies ran while one was open for 5% of the time, Pallas kernels for 23%

profile of v1, /device:TPU:0, one launch (start us, length us, event | category | flops | bytes accessed | tf_op | source)
XLA Modules:
  0.0 522.6 jit_solution(7187723058001141374)
XLA Ops:
  3.2 31.9 %attn_fwd.1 = (bf16[800,768]{1,0:T(8,128)(2,1)}, bf16[800,768]{1,0:T(8,128)(2,1)}, bf16[800,768]{1,0:T(8,128)(2,1)}, bf16[800,768]{1,0:T(8,128)(2,1)}, bf16[800,...) custom-call(s32[4]{0:T(128)} %banks.3, ...), custom_call_target="tpu_custom_call" | custom-call | tf_op jit(solution)/shard_map/attn_fwd/pallas_call | solution.py:198
  35.1 3.0 collective-permute-start.11
  38.9 27.4 %collective-permute-done.11.refs_10_.refs_6_ = bf16[800,768]{1,0:T(8,128)(2,1)} collective-permute-done((bf16[800,768]{1,0:T(8,128)(2,1)}, bf16[800,768]{1,0:T(8,128)(2,1)}, u32[]{:S(2)}, u32[]{:S(2)}) %collective-permute-start.11) | collective-permute-done | bytes 1228832 | tf_op jit(solution)/shard_map/ppermute | solution.py:602
  66.3 25.5 %collective-permute-done.13.refs_14_.refs_8_ = bf16[800,768]{1,0:T(8,128)(2,1)} collective-permute-done((bf16[800,768]{1,0:T(8,128)(2,1)S(1)}, bf16[800,768]{1,0:T(8,128)(2,1)}, u32[]{:S(2)}, u32[]{:S(2)}) %collective-permute-start.13) | collective-permute-done | bytes 1228832 | tf_op jit(solution)/shard_map/ppermute | solution.py:602
  91.9 1.7 collective-permute-start.1
  93.6 1.8 collective-permute-done.1
  97.6 1.7 collective-permute-start.4
  99.4 1.9 collective-permute-done.4
  103.6 1.7 collective-permute-start.9
  105.4 2.1 collective-permute-done.9.refs_6_.refs_4_
  112.0 48.5 %experts.3 = (f32[128,768]{1,0:T(8,128)}, f32[128,3072]{1,0:T(8,128)}, f32[128,3072]{1,0:T(8,128)}, f32[128,768]{1,0:T(8,128)}, bf16[1856,768]{1,0:T(8,128)(2,1)...) custom-call(s32[1]{0:T(128)} %bitcast.2.eidx.refs_0_, s32[4,4]{1,0:T(4,128)} %pad_add_fusion.1.refs_1_, ...), custom_call_target="tpu_custom_call" | custom-call | tf_op jit(solution)/shard_map/experts/pallas_call | solution.py:466
  165.3 1.7 collective-permute-start.34
  167.0 40.6 %experts.4 = (f32[128,768]{1,0:T(8,128)}, f32[128,3072]{1,0:T(8,128)}, f32[128,3072]{1,0:T(8,128)}, f32[128,768]{1,0:T(8,128)}, bf16[800,768]{1,0:T(8,128)(2,1)}...) custom-call(s32[1]{0:T(128)} %bitcast.2.eidx.refs_0_, ...), custom_call_target="tpu_custom_call" | custom-call | tf_op jit(solution)/shard_map/experts/pallas_call | solution.py:466
  207.6 31.0 %experts.5 = (f32[128,768]{1,0:T(8,128)}, f32[128,3072]{1,0:T(8,128)}, f32[128,3072]{1,0:T(8,128)}, f32[128,768]{1,0:T(8,128)}, bf16[800,768]{1,0:T(8,128)(2,1)}...) custom-call(s32[1]{0:T(128)} %bitcast.2.eidx.refs_0_, ...), custom_call_target="tpu_custom_call" | custom-call | tf_op jit(solution)/shard_map/experts/pallas_call | solution.py:466
  239.8 53.9 %collective-permute-start.19 = (f32[8,800]{1,0:T(8,128)S(1)}, f32[8,800]{1,0:T(8,128)S(1)}, u32[]{:S(2)}, u32[]{:S(2)}) collective-permute-start(f32[8,800]{1,0:T(8,128)S(1)} %copy-done.27), channel_id=1, source_target_pairs={{0,1},{1,0},{2,3},{3,2},{4,5},{5,4},{6,7},{7,6},{8,9},{9,8},{10,11... | collective-permute-start | bytes 76808 | tf_op jit(solution)/shard_map/ppermute | solution.py:602
  293.8 1.5 constant_dynamic-update-slice_fusion.6
  297.6 2.7 collective-permute-done.20
  302.9 17.8 %collective-permute-done.40 = bf16[64,7680]{1,0:T(8,128)(2,1)S(1)} collective-permute-done((bf16[64,7680]{1,0:T(8,128)(2,1)S(1)}, bf16[64,7680]{1,0:T(8,128)(2,1)S(1)}, u32[]{:S(2)}, u32[]{:S(2)}) %collective-permute-start.40) | collective-permute-done | bytes 983072 | tf_op jit(solution)/shard_map/ppermute | solution.py:602
  320.8 1.6 collective-permute-start.35
  323.5 1.8 collective-permute-start.23
  325.6 9.3 %collective-permute-done.35 = bf16[32,7680]{1,0:T(8,128)(2,1)S(1)} collective-permute-done((bf16[32,7680]{1,0:T(8,128)(2,1)S(1)}, bf16[32,7680]{1,0:T(8,128)(2,1)S(1)}, u32[]{:S(2)}, u32[]{:S(2)}) %collective-permute-start.35) | collective-permute-done | bytes 491552 | tf_op jit(solution)/shard_map/ppermute | solution.py:602
  334.9 1.7 collective-permute-start.17
  336.8 7.3 %collective-permute-done.41 = bf16[32,7680]{1,0:T(8,128)(2,1)S(1)} collective-permute-done((bf16[32,7680]{1,0:T(8,128)(2,1)S(1)}, bf16[32,7680]{1,0:T(8,128)(2,1)S(1)}, u32[]{:S(2)}, u32[]{:S(2)}) %collective-permute-start.41) | collective-permute-done | bytes 491552 | tf_op jit(solution)/shard_map/ppermute | solution.py:602
  344.1 2.4 collective-permute-start.36
  346.6 10.3 %collective-permute-done.36 = bf16[16,7680]{1,0:T(8,128)(2,1)S(1)} collective-permute-done((bf16[16,7680]{1,0:T(8,128)(2,1)S(1)}, bf16[16,7680]{1,0:T(8,128)(2,1)S(1)}, u32[]{:S(2)}, u32[]{:S(2)}) %collective-permute-start.36) | collective-permute-done | bytes 245792 | tf_op jit(solution)/shard_map/ppermute | solution.py:602
  357.0 3.0 collective-permute-start.37
  361.1 45.1 %attn_bwd.1 = (f32[788,768]{1,0:T(8,128)}, f32[9,128,768]{2,1,0:T(8,128)}, f32[8,128]{1,0:T(8,128)}) custom-call(s32[4]{0:T(128)} %banks.3, bf16[788,768]{1,0:T(8,128)(2,1)} %tok.3, bf16[800,768]{1,0:T(8,128)(2,1)} %copy-done.2, f32[1,768]{1,0:T(1,128)} %reshape.256.g1, f32[1,768]{1,0:T(1,128)} %reshape.257.g2, bf16[768,768]{1,0:T(8,128)(2,1)} %wq.3, ...), custom_call_target="tpu_custom_call" | custom-call | tf_op jit(solution)/shard_map/attn_bwd/pallas_call | solution.py:589
  406.2 2.2 select_maximum_fusion
  413.6 2.8 collective-permute-start.38
  416.4 7.5 %collective-permute-done.25 = bf16[296,768]{1,0:T(8,128)(2,1)S(1)} collective-permute-done((bf16[296,768]{1,0:T(8,128)(2,1)S(1)}, bf16[296,768]{1,0:T(8,128)(2,1)S(1)}, u32[]{:S(2)}, u32[]{:S(2)}) %collective-permute-start.25) | collective-permute-done | bytes 454688 | tf_op jit(solution)/shard_map/ppermute | solution.py:602
  424.1 3.6 collective-permute-start.26
  427.8 9.6 %collective-permute-start.44 = (bf16[32,7680]{1,0:T(8,128)(2,1)S(1)}, bf16[32,7680]{1,0:T(8,128)(2,1)S(1)}, u32[]{:S(2)}, u32[]{:S(2)}) collective-permute-start(bf16[32,7680]{1,0:T(8,128)(2,1)S(1)} %maximum_select_fusion.7), channel_id=1, source_target_pairs={{0,8},{4,12},{8,0},{12,4},{16,24},{20,28},{24,16},{28,20},{1,9},{5... | collective-permute-start | bytes 1474568 | tf_op jit(solution)/shard_map/ppermute | solution.py:602
  437.5 5.5 %collective-permute-start.27 = (bf16[74,768]{1,0:T(8,128)(2,1)S(1)}, bf16[74,768]{1,0:T(8,128)(2,1)S(1)}, u32[]{:S(2)}, u32[]{:S(2)}) collective-permute-start(bf16[74,768]{1,0:T(8,128)(2,1)S(1)} %dynamic-slice_convert_fusion.8), channel_id=1, source_target_pairs={{0,8},{4,12},{8,0},{12,4},{16,24},{20,28},{24,16},{28,20},{1,9},{5... | collective-permute-start | bytes 341000 | tf_op jit(solution)/shard_map/ppermute | solution.py:602
  443.1 1.8 collective-permute-start.39
  444.9 5.9 %collective-permute-done.27 = bf16[74,768]{1,0:T(8,128)(2,1)S(1)} collective-permute-done((bf16[74,768]{1,0:T(8,128)(2,1)S(1)}, bf16[74,768]{1,0:T(8,128)(2,1)S(1)}, u32[]{:S(2)}, u32[]{:S(2)}) %collective-permute-start.27) | collective-permute-done | bytes 113696 | tf_op jit(solution)/shard_map/ppermute | solution.py:602
  453.6 2.5 collective-permute-done.28
  457.5 3.3 add_convert_fusion.2
  461.4 2.3 collective-permute-start.30
  463.7 4.2 collective-permute-done.39
  468.3 1.8 collective-permute-start.31
  470.1 18.8 %collective-permute-done.45 = bf16[64,7680]{1,0:T(8,128)(2,1)S(1)} collective-permute-done((bf16[64,7680]{1,0:T(8,128)(2,1)S(1)}, bf16[64,7680]{1,0:T(8,128)(2,1)S(1)}, u32[]{:S(2)}, u32[]{:S(2)}) %collective-permute-start.45) | collective-permute-done | bytes 983072 | tf_op jit(solution)/shard_map/ppermute | solution.py:602
  489.3 2.5 collective-permute-done.31
  493.6 8.7 %collective-permute-done.32 = bf16[296,768]{1,0:T(8,128)(2,1)S(1)} collective-permute-done((bf16[296,768]{1,0:T(8,128)(2,1)S(1)}, bf16[296,768]{1,0:T(8,128)(2,1)S(1)}, u32[]{:S(2)}, u32[]{:S(2)}) %collective-permute-start.32) | collective-permute-done | bytes 454688 | tf_op jit(solution)/shard_map/ppermute | solution.py:602
  502.7 3.3 slice_bitcast_fusion
  505.9 3.5 copy.49
  509.5 2.3 maximum_convert_fusion.1
  511.8 2.3 copy.48
  514.1 1.8 fusion.2
  (171 shorter events, 45.6 us)
Async XLA Ops:
  35.1 68.5 %copy-start.16 = (f32[8,800]{1,0:T(8,128)S(1)}, f32[8,800]{1,0:T(8,128)}, u32[]{:S(2)}) copy-start(f32[8,800]{1,0:T(8,128)} %get-tuple-element.65.refs_4_.pt) | copy-start | bytes 76804
  35.1 31.2 %collective-permute-start.11 = (bf16[800,768]{1,0:T(8,128)(2,1)}, bf16[800,768]{1,0:T(8,128)(2,1)}, u32[]{:S(2)}, u32[]{:S(2)}) collective-permute-start(bf16[800,768]{1,0:T(8,128)(2,1)} %get-tuple-element.66.refs_8_.refs_6_.n2), channel_id=1, source_target_pairs={{0,2},{1,3},{2,0},{3,1},{4,6},{5,7},{6,4},{7,5},{8,10},{9,11},{10,... | collective-permute-start | bytes 3686408 | tf_op jit(solution)/shard_map/ppermute | solution.py:602
  38.3 73.2 %copy-start.2 = (bf16[800,768]{1,0:T(8,128)(2,1)}, bf16[800,768]{1,0:T(8,128)(2,1)S(1)}, u32[]{:S(2)}) copy-start(bf16[800,768]{1,0:T(8,128)(2,1)S(1)} %pad.14.refs_12_.refs_8_.cot) | copy-start | bytes 3686404
  38.3 53.6 %collective-permute-start.13 = (bf16[800,768]{1,0:T(8,128)(2,1)S(1)}, bf16[800,768]{1,0:T(8,128)(2,1)}, u32[]{:S(2)}, u32[]{:S(2)}) collective-permute-start(bf16[800,768]{1,0:T(8,128)(2,1)S(1)} %pad.14.refs_12_.refs_8_.cot), channel_id=1, source_target_pairs={{0,2},{1,3},{2,0},{3,1},{4,6},{5,7},{6,4},{7,5},{8,10},{9,11},{10,... | collective-permute-start | bytes 3686408 | tf_op jit(solution)/shard_map/ppermute | solution.py:602
  38.4 73.1 %collective-permute-start.7 = (bf16[800,768]{1,0:T(8,128)(2,1)S(1)}, bf16[800,768]{1,0:T(8,128)(2,1)}, u32[]{:S(2)}, u32[]{:S(2)}) collective-permute-start(bf16[800,768]{1,0:T(8,128)(2,1)S(1)} %copy-done.4), channel_id=1, source_target_pairs={{0,1},{1,0},{2,3},{3,2},{4,5},{5,4},{6,7},{7,6},{8,9},{9,8},{10,11... | collective-permute-start | bytes 3686408 | tf_op jit(solution)/shard_map/ppermute | solution.py:602
  38.4 73.0 %collective-permute-start.8 = (bf16[800,768]{1,0:T(8,128)(2,1)S(1)}, bf16[800,768]{1,0:T(8,128)(2,1)}, u32[]{:S(2)}, u32[]{:S(2)}) collective-permute-start(bf16[800,768]{1,0:T(8,128)(2,1)S(1)} %pad.14.refs_12_.refs_8_.cot), channel_id=1, source_target_pairs={{0,1},{1,0},{2,3},{3,2},{4,5},{5,4},{6,7},{7,6},{8,9},{9,8},{10,11... | collective-permute-start | bytes 3686408 | tf_op jit(solution)/shard_map/ppermute | solution.py:602
  66.3 45.1 %collective-permute-start.12 = (bf16[800,768]{1,0:T(8,128)(2,1)}, bf16[800,768]{1,0:T(8,128)(2,1)}, u32[]{:S(2)}, u32[]{:S(2)}) collective-permute-start(bf16[800,768]{1,0:T(8,128)(2,1)} %collective-permute-done.11.refs_10_.refs_6_), channel_id=1, source_target_pairs={{0,1},{1,0},{2,3},{3,2},{4,5},{5,4},{6,7},{7,6},{8,9},{9,8},{10,11... | collective-permute-start | bytes 3686408 | tf_op jit(solution)/shard_map/ppermute | solution.py:602
  91.9 19.6 %collective-permute-start.14 = (bf16[800,768]{1,0:T(8,128)(2,1)}, bf16[800,768]{1,0:T(8,128)(2,1)}, u32[]{:S(2)}, u32[]{:S(2)}) collective-permute-start(bf16[800,768]{1,0:T(8,128)(2,1)} %collective-permute-done.13.refs_14_.refs_8_), channel_id=1, source_target_pairs={{0,1},{1,0},{2,3},{3,2},{4,5},{5,4},{6,7},{7,6},{8,9},{9,8},{10,11... | collective-permute-start | bytes 3686408 | tf_op jit(solution)/shard_map/ppermute | solution.py:602
  91.9 3.5 collective-permute-start.1
  95.4 1.1 collective-permute-start
  96.5 1.1 collective-permute-start.2
  97.6 3.6 collective-permute-start.4
  101.3 1.2 collective-permute-start.3
  102.5 1.2 collective-permute-start.5
  103.6 3.9 collective-permute-start.9
  107.5 1.2 collective-permute-start.6
  108.7 2.7 collective-permute-start.10
  165.3 135.6 %collective-permute-start.34 = (bf16[64,7680]{1,0:T(8,128)(2,1)}, bf16[64,7680]{1,0:T(8,128)(2,1)}, u32[]{:S(2)}, u32[]{:S(2)}) collective-permute-start(bf16[64,7680]{1,0:T(8,128)(2,1)} %dynamic-slice_convert_fusion.1), channel_id=1, source_target_pairs={{0,4},{4,0},{8,12},{12,8},{16,20},{20,16},{24,28},{28,24},{1,5},{5... | collective-permute-start | bytes 2949128 | tf_op jit(solution)/shard_map/ppermute | solution.py:602
  239.8 56.6 %collective-permute-start.19 = (f32[8,800]{1,0:T(8,128)S(1)}, f32[8,800]{1,0:T(8,128)S(1)}, u32[]{:S(2)}, u32[]{:S(2)}) collective-permute-start(f32[8,800]{1,0:T(8,128)S(1)} %copy-done.27), channel_id=1, source_target_pairs={{0,1},{1,0},{2,3},{3,2},{4,5},{5,4},{6,7},{7,6},{8,9},{9,8},{10,11... | collective-permute-start | bytes 76808 | tf_op jit(solution)/shard_map/ppermute | solution.py:602
  293.7 3.5 collective-permute-start.18
  296.4 3.9 collective-permute-start.20
  296.6 24.2 %collective-permute-start.40 = (bf16[64,7680]{1,0:T(8,128)(2,1)S(1)}, bf16[64,7680]{1,0:T(8,128)(2,1)S(1)}, u32[]{:S(2)}, u32[]{:S(2)}) collective-permute-start(bf16[64,7680]{1,0:T(8,128)(2,1)S(1)} %dynamic-slice_convert_fusion), channel_id=1, source_target_pairs={{0,4},{4,0},{8,12},{12,8},{16,20},{20,16},{24,28},{28,24},{1,5},{5... | collective-permute-start | bytes 2949128 | tf_op jit(solution)/shard_map/ppermute | solution.py:602
  297.0 25.6 %collective-permute-start.22 = (bf16[800,768]{1,0:T(8,128)(2,1)S(1)}, bf16[800,768]{1,0:T(8,128)(2,1)S(1)}, u32[]{:S(2)}, u32[]{:S(2)}) collective-permute-start(bf16[800,768]{1,0:T(8,128)(2,1)S(1)} %copy-done.26), channel_id=1, source_target_pairs={{0,1},{1,0},{2,3},{3,2},{4,5},{5,4},{6,7},{7,6},{8,9},{9,8},{10,11... | collective-permute-start | bytes 3686408 | tf_op jit(solution)/shard_map/ppermute | solution.py:602
  297.2 59.8 %collective-permute-start.21 = (bf16[800,768]{1,0:T(8,128)(2,1)S(1)}, bf16[800,768]{1,0:T(8,128)(2,1)S(1)}, u32[]{:S(2)}, u32[]{:S(2)}) collective-permute-start(bf16[800,768]{1,0:T(8,128)(2,1)S(1)} %copy-done.24), channel_id=1, source_target_pairs={{0,1},{1,0},{2,3},{3,2},{4,5},{5,4},{6,7},{7,6},{8,9},{9,8},{10,11... | collective-permute-start | bytes 3686408 | tf_op jit(solution)/shard_map/ppermute | solution.py:602
  300.3 157.1 %collective-permute-start.15 = (bf16[800,768]{1,0:T(8,128)(2,1)}, bf16[800,768]{1,0:T(8,128)(2,1)}, u32[]{:S(2)}, u32[]{:S(2)}) collective-permute-start(bf16[800,768]{1,0:T(8,128)(2,1)} %get-tuple-element.75), channel_id=1, source_target_pairs={{0,1},{1,0},{2,3},{3,2},{4,5},{5,4},{6,7},{7,6},{8,9},{9,8},{10,11... | collective-permute-start | bytes 3686408 | tf_op jit(solution)/shard_map/ppermute | solution.py:602
  301.0 22.5 %collective-permute-start.16 = (bf16[800,768]{1,0:T(8,128)(2,1)S(1)}, bf16[800,768]{1,0:T(8,128)(2,1)S(1)}, u32[]{:S(2)}, u32[]{:S(2)}) collective-permute-start(bf16[800,768]{1,0:T(8,128)(2,1)S(1)} %copy-done.25), channel_id=1, source_target_pairs={{0,1},{1,0},{2,3},{3,2},{4,5},{5,4},{6,7},{7,6},{8,9},{9,8},{10,11... | collective-permute-start | bytes 3686408 | tf_op jit(solution)/shard_map/ppermute | solution.py:602
  320.8 14.1 %collective-permute-start.35 = (bf16[32,7680]{1,0:T(8,128)(2,1)S(1)}, bf16[32,7680]{1,0:T(8,128)(2,1)S(1)}, u32[]{:S(2)}, u32[]{:S(2)}) collective-permute-start(bf16[32,7680]{1,0:T(8,128)(2,1)S(1)} %dynamic-slice_convert_fusion.3), channel_id=1, source_target_pairs={{0,8},{4,12},{8,0},{12,4},{16,24},{20,28},{24,16},{28,20},{1,9},{5... | collective-permute-start | bytes 1474568 | tf_op jit(solution)/shard_map/ppermute | solution.py:602
  322.6 21.5 %collective-permute-start.41 = (bf16[32,7680]{1,0:T(8,128)(2,1)S(1)}, bf16[32,7680]{1,0:T(8,128)(2,1)S(1)}, u32[]{:S(2)}, u32[]{:S(2)}) collective-permute-start(bf16[32,7680]{1,0:T(8,128)(2,1)S(1)} %dynamic-slice_convert_fusion.2), channel_id=1, source_target_pairs={{0,8},{4,12},{8,0},{12,4},{16,24},{20,28},{24,16},{28,20},{1,9},{5... | collective-permute-start | bytes 1474568 | tf_op jit(solution)/shard_map/ppermute | solution.py:602
  323.5 36.6 %collective-permute-start.23 = (bf16[800,768]{1,0:T(8,128)(2,1)S(1)}, bf16[800,768]{1,0:T(8,128)(2,1)S(1)}, u32[]{:S(2)}, u32[]{:S(2)}) collective-permute-start(bf16[800,768]{1,0:T(8,128)(2,1)S(1)} %add_convert_fusion), channel_id=1, source_target_pairs={{0,2},{1,3},{2,0},{3,1},{4,6},{5,7},{6,4},{7,5},{8,10},{9,11},{10,... | collective-permute-start | bytes 3686408 | tf_op jit(solution)/shard_map/ppermute | solution.py:602
  334.9 122.6 %collective-permute-start.17 = (bf16[800,768]{1,0:T(8,128)(2,1)S(1)}, bf16[800,768]{1,0:T(8,128)(2,1)}, u32[]{:S(2)}, u32[]{:S(2)}) collective-permute-start(bf16[800,768]{1,0:T(8,128)(2,1)S(1)} %add_convert_fusion.1), channel_id=1, source_target_pairs={{0,2},{1,3},{2,0},{3,1},{4,6},{5,7},{6,4},{7,5},{8,10},{9,11},{10,... | collective-permute-start | bytes 3686408 | tf_op jit(solution)/shard_map/ppermute | solution.py:602
  344.1 12.9 %collective-permute-start.36 = (bf16[16,7680]{1,0:T(8,128)(2,1)S(1)}, bf16[16,7680]{1,0:T(8,128)(2,1)S(1)}, u32[]{:S(2)}, u32[]{:S(2)}) collective-permute-start(bf16[16,7680]{1,0:T(8,128)(2,1)S(1)} %dynamic-slice_convert_fusion.6), channel_id=1, source_target_pairs={{0,16},{4,20},{8,24},{12,28},{16,0},{20,4},{24,8},{28,12},{1,17},{... | collective-permute-start | bytes 737288 | tf_op jit(solution)/shard_map/ppermute | solution.py:602
  357.0 51.7 %collective-permute-start.42 = (bf16[16,7680]{1,0:T(8,128)(2,1)S(1)}, bf16[16,7680]{1,0:T(8,128)(2,1)}, u32[]{:S(2)}, u32[]{:S(2)}) collective-permute-start(bf16[16,7680]{1,0:T(8,128)(2,1)S(1)} %dynamic-slice_convert_fusion.5), channel_id=1, source_target_pairs={{0,16},{4,20},{8,24},{12,28},{16,0},{20,4},{24,8},{28,12},{1,17},{... | collective-permute-start | bytes 737288 | tf_op jit(solution)/shard_map/ppermute | solution.py:602
  357.0 55.4 %collective-permute-start.37 = (bf16[16,7680]{1,0:T(8,128)(2,1)S(1)}, bf16[16,7680]{1,0:T(8,128)(2,1)}, u32[]{:S(2)}, u32[]{:S(2)}) collective-permute-start(bf16[16,7680]{1,0:T(8,128)(2,1)S(1)} %add_convert_fusion.4), channel_id=1, source_target_pairs={{0,16},{4,20},{8,24},{12,28},{16,0},{20,4},{24,8},{28,12},{1,17},{... | collective-permute-start | bytes 737288 | tf_op jit(solution)/shard_map/ppermute | solution.py:602
  408.6 2.5 collective-permute-start.24
  409.6 18.0 %collective-permute-start.43 = (bf16[16,7680]{1,0:T(8,128)(2,1)S(1)}, bf16[16,7680]{1,0:T(8,128)(2,1)S(1)}, u32[]{:S(2)}, u32[]{:S(2)}) collective-permute-start(bf16[16,7680]{1,0:T(8,128)(2,1)S(1)} %add_convert_fusion.3), channel_id=1, source_target_pairs={{0,16},{4,20},{8,24},{12,28},{16,0},{20,4},{24,8},{28,12},{1,17},{... | collective-permute-start | bytes 737288 | tf_op jit(solution)/shard_map/ppermute | solution.py:602
  411.4 12.5 %collective-permute-start.25 = (bf16[296,768]{1,0:T(8,128)(2,1)S(1)}, bf16[296,768]{1,0:T(8,128)(2,1)S(1)}, u32[]{:S(2)}, u32[]{:S(2)}) collective-permute-start(bf16[296,768]{1,0:T(8,128)(2,1)S(1)} %dynamic-slice_convert_fusion.4), channel_id=1, source_target_pairs={{0,2},{1,3},{2,0},{3,1},{4,6},{5,7},{6,4},{7,5},{8,10},{9,11},{10,... | collective-permute-start | bytes 1363976 | tf_op jit(solution)/shard_map/ppermute | solution.py:602
  413.6 29.3 %collective-permute-start.38 = (bf16[32,7680]{1,0:T(8,128)(2,1)S(1)}, bf16[32,7680]{1,0:T(8,128)(2,1)S(1)}, u32[]{:S(2)}, u32[]{:S(2)}) collective-permute-start(bf16[32,7680]{1,0:T(8,128)(2,1)S(1)} %maximum_select_fusion.6), channel_id=1, source_target_pairs={{0,8},{4,12},{8,0},{12,4},{16,24},{20,28},{24,16},{28,20},{1,9},{5... | collective-permute-start | bytes 1474568 | tf_op jit(solution)/shard_map/ppermute | solution.py:602
  424.1 13.3 %collective-permute-start.26 = (bf16[148,768]{1,0:T(8,128)(2,1)S(1)}, bf16[148,768]{1,0:T(8,128)(2,1)S(1)}, u32[]{:S(2)}, u32[]{:S(2)}) collective-permute-start(bf16[148,768]{1,0:T(8,128)(2,1)S(1)} %dynamic-slice_convert_fusion.7), channel_id=1, source_target_pairs={{0,4},{4,0},{8,12},{12,8},{16,20},{20,16},{24,28},{28,24},{1,5},{5... | collective-permute-start | bytes 681992 | tf_op jit(solution)/shard_map/ppermute | solution.py:602
  427.8 24.4 %collective-permute-start.44 = (bf16[32,7680]{1,0:T(8,128)(2,1)S(1)}, bf16[32,7680]{1,0:T(8,128)(2,1)S(1)}, u32[]{:S(2)}, u32[]{:S(2)}) collective-permute-start(bf16[32,7680]{1,0:T(8,128)(2,1)S(1)} %maximum_select_fusion.7), channel_id=1, source_target_pairs={{0,8},{4,12},{8,0},{12,4},{16,24},{20,28},{24,16},{28,20},{1,9},{5... | collective-permute-start | bytes 1474568 | tf_op jit(solution)/shard_map/ppermute | solution.py:602
  437.5 13.3 %collective-permute-start.27 = (bf16[74,768]{1,0:T(8,128)(2,1)S(1)}, bf16[74,768]{1,0:T(8,128)(2,1)S(1)}, u32[]{:S(2)}, u32[]{:S(2)}) collective-permute-start(bf16[74,768]{1,0:T(8,128)(2,1)S(1)} %dynamic-slice_convert_fusion.8), channel_id=1, source_target_pairs={{0,8},{4,12},{8,0},{12,4},{16,24},{20,28},{24,16},{28,20},{1,9},{5... | collective-permute-start | bytes 341000 | tf_op jit(solution)/shard_map/ppermute | solution.py:602
  443.1 24.8 %collective-permute-start.39 = (bf16[64,7680]{1,0:T(8,128)(2,1)S(1)}, bf16[64,7680]{1,0:T(8,128)(2,1)S(1)}, u32[]{:S(2)}, u32[]{:S(2)}) collective-permute-start(bf16[64,7680]{1,0:T(8,128)(2,1)S(1)} %maximum_select_fusion.3), channel_id=1, source_target_pairs={{0,4},{4,0},{8,12},{12,8},{16,20},{20,16},{24,28},{28,24},{1,5},{5... | collective-permute-start | bytes 2949128 | tf_op jit(solution)/shard_map/ppermute | solution.py:602
  450.9 5.2 collective-permute-start.28
  452.4 36.6 %collective-permute-start.45 = (bf16[64,7680]{1,0:T(8,128)(2,1)S(1)}, bf16[64,7680]{1,0:T(8,128)(2,1)S(1)}, u32[]{:S(2)}, u32[]{:S(2)}) collective-permute-start(bf16[64,7680]{1,0:T(8,128)(2,1)S(1)} %maximum_select_fusion.4), channel_id=1, source_target_pairs={{0,4},{4,0},{8,12},{12,8},{16,20},{20,16},{24,28},{28,24},{1,5},{5... | collective-permute-start | bytes 2949128 | tf_op jit(solution)/shard_map/ppermute | solution.py:602
  456.1 5.2 collective-permute-start.29
  461.4 6.9 %collective-permute-start.30 = (bf16[74,768]{1,0:T(8,128)(2,1)S(1)}, bf16[74,768]{1,0:T(8,128)(2,1)S(1)}, u32[]{:S(2)}, u32[]{:S(2)}) collective-permute-start(bf16[74,768]{1,0:T(8,128)(2,1)S(1)} %maximum_select_fusion.10), channel_id=1, source_target_pairs={{0,8},{4,12},{8,0},{12,4},{16,24},{20,28},{24,16},{28,20},{1,9},{5... | collective-permute-start | bytes 341000 | tf_op jit(solution)/shard_map/ppermute | solution.py:602
  468.3 23.5 %collective-permute-start.31 = (bf16[148,768]{1,0:T(8,128)(2,1)S(1)}, bf16[148,768]{1,0:T(8,128)(2,1)S(1)}, u32[]{:S(2)}, u32[]{:S(2)}) collective-permute-start(bf16[148,768]{1,0:T(8,128)(2,1)S(1)} %maximum_select_fusion.9), channel_id=1, source_target_pairs={{0,4},{4,0},{8,12},{12,8},{16,20},{20,16},{24,28},{28,24},{1,5},{5... | collective-permute-start | bytes 681992 | tf_op jit(solution)/shard_map/ppermute | solution.py:602
  491.9 10.3 %collective-permute-start.32 = (bf16[296,768]{1,0:T(8,128)(2,1)S(1)}, bf16[296,768]{1,0:T(8,128)(2,1)S(1)}, u32[]{:S(2)}, u32[]{:S(2)}) collective-permute-start(bf16[296,768]{1,0:T(8,128)(2,1)S(1)} %maximum_select_fusion.8), channel_id=1, source_target_pairs={{0,2},{1,3},{2,0},{3,1},{4,6},{5,7},{6,4},{7,5},{8,10},{9,11},{10,... | collective-permute-start | bytes 1363976 | tf_op jit(solution)/shard_map/ppermute | solution.py:602
  502.6 11.4 %collective-permute-start.33 = (bf16[592,768]{1,0:T(8,128)(2,1)S(1)}, bf16[592,768]{1,0:T(8,128)(2,1)}, u32[]{:S(2)}, u32[]{:S(2)}) collective-permute-start(bf16[592,768]{1,0:T(8,128)(2,1)S(1)} %maximum_select_fusion.5), channel_id=1, source_target_pairs={{0,1},{1,0},{2,3},{3,2},{4,5},{5,4},{6,7},{7,6},{8,9},{9,8},{10,11... | collective-permute-start | bytes 2727944 | tf_op jit(solution)/shard_map/ppermute | solution.py:602
  (26 other events, 330.4 us)

commit v2 on v1

v2 whole, which is shorter than its diff:
```python
import functools
import math

import jax
import jax.numpy as jnp
from jax import lax
from jax.experimental import pallas as pl
from jax.experimental.pallas import tpu as pltpu
from jax.sharding import PartitionSpec as P

HEAD_DIM = 64
RANK = 16
SEQ = 197
EPS = 1e-06
BF = jnp.bfloat16
F32 = jnp.float32
I32 = jnp.int32
LOG2E = math.log2(math.e)
SCALE2 = HEAD_DIM ** (-0.5) * LOG2E
NEG = -1e30
CHUNK = 1536
VMEM = pl.BlockSpec(memory_space=pltpu.VMEM)
SMEM = pl.BlockSpec(memory_space=pltpu.SMEM)
ANY = pl.BlockSpec(memory_space=pl.ANY)


def nn(a, b):
    return jnp.dot(a, b, preferred_element_type=F32)


def nt(a, b):
    return lax.dot_general(a, b, (((1,), (1,)), ((), ())), preferred_element_type=F32)


def tn(a, b):
    return lax.dot_general(a, b, (((0,), (0,)), ((), ())), preferred_element_type=F32)


def params(mib):
    return pltpu.CompilerParams(vmem_limit_bytes=mib * 1024 * 1024)


def cost(us):
    return pl.CostEstimate(
        flops=int(us * 1.1e9), bytes_accessed=int(us * 3e6), transcendentals=0
    )


def split_parts(x, n):
    parts = []
    for _ in range(n):
        low = x.astype(BF)
        parts.append(low)
        x = x - low.astype(F32)
    return parts


def store_lines(ref, start, lines, n):
    d = ref.shape[1]
    for i, part in enumerate(split_parts(lines, n)):
        part = part.astype(F32)
        rest = part.shape[1] - d
        tail = jnp.concatenate(
            [part[:, d:], jnp.zeros((part.shape[0], d - rest), F32)], axis=1
        )
        ref[start + 16 * i : start + 16 * i + 16, :] = jnp.concatenate(
            [part[:, :d], tail], axis=0
        ).astype(BF)


def load_lines(block, rest, n):
    total = sum(block[16 * i : 16 * i + 16, :] for i in range(n))
    return jnp.concatenate([total[:8], total[8:, :rest]], axis=1)


def image_banks(banks, row, images):
    bank = jnp.full(row.shape, banks[0], I32)
    for i in range(1, images):
        bank = jnp.where(row >= SEQ * i, banks[i], bank)
    return bank


def bank_mask(banks, start, count, images, width):
    row = lax.broadcasted_iota(I32, (count, width), 0) + start
    col = lax.broadcasted_iota(I32, (count, width), 1)
    return (col // RANK == image_banks(banks, row, images)).astype(F32)


def norm_parts(x):
    mean = jnp.mean(x, axis=-1, keepdims=True)
    cen = x - mean
    rstd = lax.rsqrt(jnp.mean(cen * cen, axis=-1, keepdims=True) + EPS)
    return cen * rstd, rstd


def norm_back(xhat, rstd, gain, grad):
    gy = grad * gain
    return rstd * (
        gy
        - jnp.mean(gy, axis=-1, keepdims=True)
        - xhat * jnp.mean(gy * xhat, axis=-1, keepdims=True)
    )


def attn_fwd_kernel(
    banks, tok, g1, wq, wk, wv, aq, bq, ak, bk, av, bv,
    n1_o, q_o, k_o, v_o, lq_o, lk_o, lv_o, att_o, lse_o,
    tokp, lset,
):
    rows = tok.shape[0]
    rp = n1_o.shape[0]
    images = rows // SEQ
    d = tok.shape[1]
    width = aq.shape[1]
    win = lse_o.shape[2]
    step_rows = 16 * (SEQ // 16)
    tokp[pl.ds(rp - 16, 16), :] = jnp.zeros((16, d), BF)
    tokp[0:rows, :] = tok[...]

    def ln1(i, _):
        r = pl.multiple_of(i * 32, 32)
        xhat, _r = norm_parts(tokp[pl.ds(r, 32), :].astype(F32))
        n1_o[pl.ds(r, 32), :] = (g1[...] * xhat).astype(BF)
        return 0

    lax.fori_loop(0, rp // 32, ln1, 0)
    half = rp // 2

    def qkv(i, _):
        r = pl.multiple_of(i * half, 16)
        x = n1_o[pl.ds(r, half), :]
        mask = bank_mask(banks, r, half, images, width)
        for w, a, b, out, low in (
            (wq, aq, bq, q_o, lq_o),
            (wk, ak, bk, k_o, lk_o),
            (wv, av, bv, v_o, lv_o),
        ):
            u = (nn(x, a[...]) * mask).astype(BF)
            low[pl.ds(r, half), :] = u
            out[pl.ds(r, half), :] = (nn(x, w[...]) + nn(u, b[...])).astype(BF)
        return 0

    lax.fori_loop(0, 2, qkv, 0)

    lane = lax.broadcasted_iota(I32, (win, 128), 1)
    first = lane < HEAD_DIM
    row_i = lax.broadcasted_iota(I32, (win, 128), 0)
    keys_i = lax.broadcasted_iota(I32, (win, win), 1)

    def image(i, _):
        off = pl.multiple_of(i * step_rows, 64)
        lo = i * (SEQ - step_rows)
        bias = jnp.where((keys_i >= lo) & (keys_i < lo + SEQ), 0.0, NEG)
        keep = row_i < lo
        lset[...] = jnp.zeros_like(lset)
        lse_tile = jnp.zeros((win, 128), F32)
        for p in range(d // 128):
            cols = slice(p * 128, p * 128 + 128)
            qp = q_o[pl.ds(off, win), cols]
            kp = k_o[pl.ds(off, win), cols]
            vp = v_o[pl.ds(off, win), cols]
            outs = []
            for h in range(2):
                mine = first if h == 0 else jnp.logical_not(first)
                qm = jnp.where(mine, qp, jnp.zeros_like(qp))
                s = nt(qm, kp) * SCALE2 + bias
                top = jnp.max(s, axis=-1, keepdims=True)
                e = jnp.exp2(s - top)
                den = jnp.sum(e, axis=-1, keepdims=True)
                w = (e * pl.reciprocal(den)).astype(BF)
                outs.append(nn(w, vp))
                lse = top + jnp.log2(den)
                lse_tile = jnp.where(lane == 2 * p + h, lse, lse_tile)
            new = jnp.where(first, outs[0], outs[1]).astype(BF)
            att_o[pl.ds(off, win), cols] = jnp.where(keep, att_o[pl.ds(off, win), cols], new)
        lset[0:win, :] = lse_tile
        lse_o[i] = jnp.transpose(lset[...])[0 : lse_o.shape[1], 0:win]
        return 0

    lax.fori_loop(0, images, image, 0)


def out_fwd_kernel(
    banks, tok, g2, att, wo, ao, bo, rwt, ra, rbt, *rest
):
    lo_o, mid_o, n2_o, lr_o, pt_o, tokp = rest[-6:]
    rows, d = tok.shape
    rp = att.shape[0]
    images = rows // SEQ
    width = ao.shape[1]
    half = rp // 2
    tokp[pl.ds(rp - 16, 16), :] = jnp.zeros((16, d), BF)
    tokp[0:rows, :] = tok[...]

    def out_proj(i, _):
        r = pl.multiple_of(i * half, 16)
        x = att[pl.ds(r, half), :]
        mask = bank_mask(banks, r, half, images, width)
        u = (nn(x, ao[...]) * mask).astype(BF)
        lo_o[pl.ds(r, half), :] = u
        mid_o[pl.ds(r, half), :] = (
            tokp[pl.ds(r, half), :].astype(F32) + nn(x, wo[...]) + nn(u, bo[...])
        )
        return 0

    lax.fori_loop(0, 2, out_proj, 0)

    def ln2(i, _):
        r = pl.multiple_of(i * 32, 32)
        xhat, _r = norm_parts(mid_o[pl.ds(r, 32), :])
        n2_o[pl.ds(r, 32), :] = (g2[...] * xhat).astype(BF)
        return 0

    lax.fori_loop(0, rp // 32, ln2, 0)
    x = n2_o[0:rp, :]
    u = (nn(x, ra[...]) * bank_mask(banks, 0, rp, images, width)).astype(BF)
    lr_o[...] = u
    logits = nt(rwt[...], x) + nt(rbt[...], u)
    e = jnp.exp(logits - jnp.max(logits, axis=0, keepdims=True))
    probs = e / jnp.sum(e, axis=0, keepdims=True)
    pt_o[...] = probs
    store_lines(n2_o, rp, probs, 3)


def attn_forward(banks, tok, g1, ws):
    rows, d = tok.shape
    rp = 32 * (-(-rows // 32))
    images = rows // SEQ
    step_rows = 16 * (SEQ // 16)
    win = rp - step_rows * (images - 1)
    width = ws[3].shape[1]
    heads_pad = 16 * (-(-d // (16 * HEAD_DIM)))
    bfd = jax.ShapeDtypeStruct((rp, d), BF)
    low = jax.ShapeDtypeStruct((rp, width), BF)
    out_shape = (bfd, bfd, bfd, bfd, low, low, low, bfd) + (
        jax.ShapeDtypeStruct((images, heads_pad, win), F32),
    )
    return pl.pallas_call(
        attn_fwd_kernel,
        out_shape=out_shape,
        in_specs=[SMEM] + [VMEM] * 11,
        out_specs=tuple([VMEM] * len(out_shape)),
        scratch_shapes=[pltpu.VMEM((rp, d), BF), pltpu.VMEM((256, 128), F32)],
        compiler_params=params(56),
        cost_estimate=cost(25),
        name="attn_fwd",
    )(banks, tok, g1, *ws)


def out_forward(banks, tok, g2, att, ws, after):
    rows, d = tok.shape
    rp = att.shape[0]
    low = jax.ShapeDtypeStruct((rp, ws[1].shape[1]), BF)
    out_shape = (
        low,
        jax.ShapeDtypeStruct((rp, d), F32),
        jax.ShapeDtypeStruct((rp + 48, d), BF),
        low,
        jax.ShapeDtypeStruct((ws[3].shape[0], rp), F32),
    )
    return pl.pallas_call(
        out_fwd_kernel,
        out_shape=out_shape,
        in_specs=[SMEM] + [VMEM] * 9 + [ANY] * len(after),
        out_specs=tuple([VMEM] * len(out_shape)),
        scratch_shapes=[pltpu.VMEM((rp, d), BF)],
        compiler_params=params(32),
        cost_estimate=cost(9),
        name="out_fwd",
    )(banks, tok, g2, att, *ws, *after)


def tables_kernel(eidx, routes, posr_o, posc_o):
    groups, _, rp = routes.shape
    local = posr_o.shape[0] // groups
    row = lax.broadcasted_iota(I32, (rp, rp), 0)
    col = lax.broadcasted_iota(I32, (rp, rp), 1)
    upper = (row < col).astype(BF)
    upper_inc = (row <= col).astype(BF)
    lower = (col < row).astype(BF)
    lower_inc = (col <= row).astype(BF)
    which = lax.broadcasted_iota(I32, (groups * local, rp), 0)
    hot = jnp.zeros((groups * local, rp), F32)
    for s in range(groups):
        r0 = routes[s, 0:1, :]
        r1 = routes[s, 1:2, :]
        for j in range(local):
            e = eidx[0] * local + j
            hit = ((r0 == e) | (r1 == e)).astype(F32)
            hot = jnp.where(which == s * local + j, hit, hot)
    hb = hot.astype(BF)
    before = nn(hb, upper)
    with_own = nn(hb, upper_inc)
    posr_o[...] = jnp.where(with_own > before, before, -1.0)
    before = nt(lower, hb)
    with_own = nt(lower_inc, hb)
    posc_o[...] = jnp.where(with_own > before, before, -1.0)


def routing_tables(eidx, routes, local):
    groups, _, rp = routes.shape
    n = groups * local
    return pl.pallas_call(
        tables_kernel,
        out_shape=(jax.ShapeDtypeStruct((n, rp), F32), jax.ShapeDtypeStruct((rp, n), F32)),
        in_specs=[SMEM, VMEM],
        out_specs=(VMEM, VMEM),
        compiler_params=params(32),
        cost_estimate=cost(2),
        name="routing_tables",
    )(eidx, routes)


def gelu_parts(x):
    e = jnp.exp2((-0.5 * LOG2E) * (x * x))
    t = pl.reciprocal(1.0 + (0.3275911 / math.sqrt(2.0)) * jnp.abs(x))
    poly = 1.061405429 * 0.5
    for c in (-1.453152027, 1.421413741, -0.284496736, 0.254829592):
        poly = poly * t + 0.5 * c
    q = poly * t * e
    phi = jnp.where(x >= 0.0, 1.0 - q, q)
    return x * phi, phi + x * (e * (1.0 / math.sqrt(2.0 * math.pi)))


def slot_count(posr, row):
    n = jnp.sum((posr[row : row + 1, :] >= 0.0).astype(F32)).astype(I32)
    return ((n + 15) // 16) * 16


def expert_kernel(cfg, *refs):
    j, sources, has_acc, merge, cap, local, experts = cfg
    n = len(sources)
    refs = list(refs)
    take = lambda k: [refs.pop(0) for _ in range(k)]
    (eidx,) = take(1)
    posr, meta = take(2)
    nrows = take(n)
    crows = take(n)
    upw, upa, upb, dnw, dna, dnb = take(6)
    if has_acc:
        (acc_in,) = take(1)
    if merge:
        posc, ret_in, grow_in, gg_in = take(4)
    (acc,) = take(1)
    if merge:
        grow_o = take(n)
        mix_o = take(n)
    else:
        ret_b, grow_b, gg_o = take(3)
    up, ua, dn, db, xbuf, cbuf, gate_b, mask_b, gg_b, hid, dgl, sems = take(12)
    if merge:
        ret_b, grow_b, ret0, grow0 = take(4)
    rp = posr.shape[1]
    d = upw.shape[1]
    ff = upw.shape[2]
    width = upa.shape[2]
    loads = [
        pltpu.make_async_copy(upa.at[j], ua, sems.at[0]),
        pltpu.make_async_copy(upw.at[j], up.at[0:d], sems.at[1]),
        pltpu.make_async_copy(upb.at[j], up.at[d : d + width], sems.at[2]),
        pltpu.make_async_copy(dnw.at[j], dn.at[:, 0:d], sems.at[3]),
        pltpu.make_async_copy(dna.at[j], dn.at[:, d : d + width], sems.at[4]),
        pltpu.make_async_copy(dnb.at[j], db, sems.at[5]),
    ]
    if has_acc:
        loads.append(pltpu.make_async_copy(acc_in, acc, sems.at[6]))
    if merge:
        loads.append(pltpu.make_async_copy(ret_in, ret0, sems.at[7]))
        loads.append(pltpu.make_async_copy(grow_in, grow0, sems.at[8]))
    for load in loads:
        load.start()
    if not has_acc:
        acc[...] = jnp.zeros_like(acc)
    slot_r = lax.broadcasted_iota(I32, (cap, rp), 0).astype(F32)
    mine = lax.broadcasted_iota(I32, (experts, rp), 0) == eidx[0] * local + j
    col_bank = (lax.broadcasted_iota(I32, (cap, width), 1) // RANK).astype(F32)
    offs = []
    off = jnp.int32(0)
    for i, s in enumerate(sources):
        off = pl.multiple_of(off, 16)
        offs.append(off)
        hit = posr[s * local + j : s * local + j + 1, :] == slot_r
        probs = load_lines(nrows[i][rp : rp + 48, :].astype(F32), rp - d, 3)
        gate_line = jnp.sum(jnp.where(mine, probs, 0.0), axis=0, keepdims=True)
        bank = meta[s, 2:3, :].astype(F32)
        gate = jnp.sum(jnp.where(hit, gate_line, 0.0), axis=1, keepdims=True)
        slot_bank = jnp.sum(jnp.where(hit, bank, 0.0), axis=1, keepdims=True)
        pick = hit.astype(F32).astype(BF)
        xbuf[pl.ds(off, cap), :] = nn(pick, nrows[i][0:rp, :]).astype(BF)
        cbuf[pl.ds(off, cap), :] = nn(pick, crows[i][...]).astype(BF)
        gate_b[pl.ds(off, cap), :] = jnp.broadcast_to(gate, (cap, 128))
        mask_b[pl.ds(off, cap), :] = (col_bank == slot_bank).astype(F32)
        off = off + slot_count(posr, s * local + j)
    total = off
    rest = pl.ds(pl.multiple_of(offs[-1] + cap, 16), cap)
    xbuf[rest, :] = jnp.zeros((cap, d), BF)
    cbuf[rest, :] = jnp.zeros((cap, d), BF)
    gate_b[rest, :] = jnp.zeros((cap, 128), F32)
    mask_b[rest, :] = jnp.zeros((cap, width), F32)
    tiles = (total + cap - 1) // cap
    chunks = [slice(c, min(c + CHUNK, ff)) for c in range(0, ff, CHUNK)]
    for load in loads:
        load.wait()

    def tile(t, _):
        rs = pl.ds(pl.multiple_of(t * cap, 16), cap)
        x = xbuf[rs, :]
        m = mask_b[rs, :]
        u = (nn(x, ua[...]) * m).astype(BF)
        xu = jnp.concatenate([x, u], axis=1)
        out = jnp.zeros((cap, d + width), F32)
        for cs in chunks:
            h, dg = gelu_parts(nn(xu, up[:, cs]))
            hb = h.astype(BF)
            hid[:, cs] = hb
            dgl[:, cs] = dg
            out = out + nn(hb, dn[cs, :])
        ud = (out[:, d:] * m).astype(BF)
        ret = (out[:, :d] + nn(ud, db[...])).astype(BF).astype(F32)
        cot = cbuf[rs, :].astype(F32)
        gate = gate_b[rs, 0:1]
        gg_b[rs, :] = jnp.broadcast_to(jnp.sum(cot * ret, axis=1, keepdims=True), (cap, 128))
        ret_b[rs, :] = (gate * ret).astype(BF)
        g = (gate * cot).astype(BF)
        gud = (nt(g, db[...]) * m).astype(BF)
        acc[:, d + 2 * ff :] += tn(ud, g)
        gg = jnp.concatenate([g, gud], axis=1)
        gr = jnp.zeros((cap, d + width), F32)
        for cs in chunks:
            gp = (nt(gg, dn[cs, :]) * dgl[:, cs]).astype(BF)
            gr = gr + nt(gp, up[:, cs])
            acc[:, d + cs.start : d + cs.stop] += tn(u, gp)
            acc[:, d + ff + cs.start : d + ff + cs.stop] += tn(gud, hid[:, cs])
        guu = (gr[:, d:] * m).astype(BF)
        acc[:, 0:d] += tn(guu, x)
        grow_b[rs, :] = (gr[:, :d] + nt(guu, ua[...])).astype(BF)
        return 0

    lax.fori_loop(0, tiles, tile, 0)
    done = pl.ds(pl.multiple_of(tiles * cap, 16), cap)
    ret_b[done, :] = jnp.zeros((cap, d), BF)
    grow_b[done, :] = jnp.zeros((cap, d), BF)
    gg_b[done, :] = jnp.zeros((cap, 128), F32)
    gg_lines = []
    for i, s in enumerate(sources):
        hit = posr[s * local + j : s * local + j + 1, :] == slot_r
        col = gg_b[pl.ds(offs[i], cap), 0:1]
        gg_lines.append(jnp.sum(jnp.where(hit, col, 0.0), axis=0, keepdims=True))
    if not merge:
        for i in range(n):
            gg_o[i : i + 1, :] = gg_lines[i]
    else:
        slot_c = lax.broadcasted_iota(I32, (rp, cap), 1).astype(F32)
        expert_row = lax.broadcasted_iota(I32, (experts, rp), 0)
        off0 = jnp.int32(0)
        for i, s in enumerate(sources):
            r0 = pl.ds(pl.multiple_of(off0, 16), cap)
            r1 = pl.ds(offs[i], cap)
            p0 = (posc[:, s * local : s * local + 1] == slot_c).astype(F32).astype(BF)
            p1 = (posc[:, s * local + 1 : s * local + 2] == slot_c).astype(F32).astype(BF)
            pick = jnp.concatenate([p0, p1], axis=1)
            for b0, b1, result in ((grow0, grow_b, grow_o[i]), (ret0, ret_b, mix_o[i])):
                both = jnp.concatenate([b0[r0, :], b1[r1, :]], axis=0)
                result[0:rp, :] = nn(pick, both).astype(BF)
            gg = jnp.where(
                expert_row == eidx[0] * local,
                gg_in[i : i + 1, :],
                jnp.where(expert_row == eidx[0] * local + 1, gg_lines[i], 0.0),
            )
            store_lines(grow_o[i], rp, gg, 2)
            off0 = off0 + slot_count(posr, s * local)


def expert_call(j, sources, eidx, tables, nrows, crows, ws, cap, acc, first=None):
    posr, posc, meta = tables
    rp, d = crows[0].shape
    local, _, ff = ws[0].shape
    width = ws[1].shape[2]
    n = len(sources)
    experts = local * lax.axis_size("expert")
    merge = first is not None
    cfg = (j, tuple(sources), acc is not None, merge, cap, local, experts)
    buf = (n + 1) * cap
    args = [eidx, posr, meta]
    args += [nrows[s] for s in sources] + [crows[s] for s in sources] + list(ws)
    in_specs = [SMEM] + [VMEM] * (2 + 2 * n) + [ANY] * 6
    if acc is not None:
        args.append(acc)
        in_specs.append(ANY)
    if merge:
        args += [posc, *first]
        in_specs += [VMEM, ANY, ANY, VMEM]
    wide = (width, 2 * d + 2 * ff)
    out_shape = (jax.ShapeDtypeStruct(wide, F32),)
    if merge:
        out_shape += (jax.ShapeDtypeStruct((rp + 32, d), BF),) * n
        out_shape += (jax.ShapeDtypeStruct((rp, d), BF),) * n
    else:
        out_shape += (jax.ShapeDtypeStruct((buf, d), BF),) * 2
        out_shape += (jax.ShapeDtypeStruct((n, rp), F32),)
    scratch = [
        pltpu.VMEM((d + width, ff), BF),
        pltpu.VMEM((d, width), BF),
        pltpu.VMEM((ff, d + width), BF),
        pltpu.VMEM((width, d), BF),
        pltpu.VMEM((buf, d), BF),
        pltpu.VMEM((buf, d), BF),
        pltpu.VMEM((buf, 128), F32),
        pltpu.VMEM((buf, width), F32),
        pltpu.VMEM((buf, 128), F32),
        pltpu.VMEM((cap, ff), BF),
        pltpu.VMEM((cap, ff), F32),
        pltpu.SemaphoreType.DMA((9,)),
    ]
    if merge:
        scratch += [pltpu.VMEM((buf, d), BF)] * 4
    return pl.pallas_call(
        functools.partial(expert_kernel, cfg),
        out_shape=out_shape,
        in_specs=in_specs,
        out_specs=(VMEM,) * len(out_shape),
        scratch_shapes=scratch,
        compiler_params=params(56 if merge else 44),
        cost_estimate=cost(30),
        name=f"expert{j}_{'far' if sources[0] else 'near'}",
    )(*args)


def out_bwd_kernel(
    banks, cot, g2, att, lo, mid, n2, lr, pt, wo, ao, bo, rwt, ra, rbt, p0, p1, p2,
    gmid, ga, gr_o,
    gml,
):
    rp, d = cot.shape
    experts = pt.shape[0]
    images = banks.shape[0]
    width = ao.shape[1]
    probs = pt[...]
    lines = sum(p[rp : rp + 32, :].astype(F32) for p in (p0, p1, p2))
    gp = load_lines(lines, rp - d, 2)
    glt = (probs * (gp - jnp.sum(gp * probs, axis=0, keepdims=True))).astype(BF)
    rb = jnp.concatenate([nn(glt, lr[...]), jnp.zeros((experts, d - width), F32)], axis=1)
    rb = jnp.concatenate([rb, jnp.zeros((32 - experts, d), F32)], axis=0)
    gr_o[3 * width : 3 * width + 32, :] = rb.astype(BF)
    mask = bank_mask(banks, 0, rp, images, width)
    gu = (tn(glt, rbt[...]) * mask).astype(BF)
    gr_o[2 * width : 3 * width, :] = tn(gu, n2[0:rp, :]).astype(BF)
    gmid[...] = tn(glt, rwt[...]) + nt(gu, ra[...])

    def ln2(i, _):
        rs = pl.ds(pl.multiple_of(i * 32, 32), 32)
        grad = gmid[rs, :] + (p0[rs, :].astype(F32) + p1[rs, :].astype(F32) + p2[rs, :].astype(F32))
        xhat, rstd = norm_parts(mid[rs, :])
        g = cot[rs, :].astype(F32) + norm_back(xhat, rstd, g2[...], grad)
        gmid[rs, :] = g
        gml[rs, :] = g.astype(BF)
        return 0

    lax.fori_loop(0, rp // 32, ln2, 0)
    g = gml[...]
    gr_o[width : 2 * width, :] = tn(lo[...], g).astype(BF)
    gu = (nt(g, bo[...]) * mask).astype(BF)
    gr_o[0:width, :] = tn(gu, att[...]).astype(BF)
    ga[...] = (nt(g, wo[...]) + nt(gu, ao[...])).astype(BF)


def out_backward(banks, cot, g2, kept, ws, parts):
    rp, d = cot.shape
    width = ws[1].shape[1]
    return pl.pallas_call(
        out_bwd_kernel,
        out_shape=(
            jax.ShapeDtypeStruct((rp, d), F32),
            jax.ShapeDtypeStruct((rp, d), BF),
            jax.ShapeDtypeStruct((3 * width + 32, d), BF),
        ),
        in_specs=[SMEM] + [VMEM] * 17,
        out_specs=(VMEM,) * 3,
        scratch_shapes=[pltpu.VMEM((rp, d), BF)],
        compiler_params=params(48),
        cost_estimate=cost(14),
        name="out_bwd",
    )(banks, cot, g2, *kept, *ws, *parts)


def attn_bwd_kernel(
    banks, n1, q, k, v, lq, lk, lv, lse, ga, bq, bk, bv,
    gq, gk, gv, uq, uk, uv, gr_o,
):
    rp, d = n1.shape
    images = banks.shape[0]
    width = bq.shape[0]
    win = lse.shape[2]
    step_rows = 16 * (SEQ // 16)
    lane = lax.broadcasted_iota(I32, (win, 128), 1)
    first = lane < HEAD_DIM
    row_i = lax.broadcasted_iota(I32, (win, 128), 0)
    key_i = lax.broadcasted_iota(I32, (win, win), 0)
    query_i = lax.broadcasted_iota(I32, (win, win), 1)

    def image(i, _):
        off = pl.multiple_of(i * step_rows, 64)
        start = i * (SEQ - step_rows)
        bias = jnp.where(
            (key_i >= start) & (key_i < start + SEQ) & (query_i >= start) & (query_i < start + SEQ),
            0.0,
            NEG,
        )
        keep = row_i < start
        ws = pl.ds(off, win)
        for p in range(d // 128):
            cols = slice(p * 128, p * 128 + 128)
            qp = q[ws, cols]
            kp = k[ws, cols]
            vp = v[ws, cols]
            gap = ga[ws, cols]
            rq, rk, rv = [], [], []
            for h in range(2):
                mine = first if h == 0 else jnp.logical_not(first)
                km = jnp.where(mine, kp, jnp.zeros_like(kp))
                vm = jnp.where(mine, vp, jnp.zeros_like(vp))
                prob = jnp.exp2(
                    nt(km, qp) * SCALE2 + bias - lse[i, 2 * p + h : 2 * p + h + 1, :]
                )
                gw = nt(vm, gap)
                delta = jnp.sum(gw * prob, axis=0, keepdims=True)
                gs = (prob * (gw - delta)).astype(BF)
                rv.append(nn(prob.astype(BF), gap))
                rk.append(nn(gs, qp))
                rq.append(tn(gs, kp))
            for parts, ref, scale in ((rq, gq, 0.125), (rk, gk, 0.125), (rv, gv, 1.0)):
                new = (jnp.where(first, parts[0], parts[1]) * scale).astype(BF)
                ref[ws, cols] = jnp.where(keep, ref[ws, cols], new)
        return 0

    lax.fori_loop(0, images, image, 0)
    x = n1[...]
    mask = bank_mask(banks, 0, rp, images, width)
    for i, (grad, low, b, u) in enumerate(((gq, lq, bq, uq), (gk, lk, bk, uk), (gv, lv, bv, uv))):
        g = grad[...]
        gr_o[(2 * i + 1) * width : (2 * i + 2) * width, :] = tn(low[...], g).astype(BF)
        gu = (nt(g, b[...]) * mask).astype(BF)
        u[...] = gu
        gr_o[2 * i * width : (2 * i + 1) * width, :] = tn(gu, x).astype(BF)


def attn_backward(banks, kept, ga, bs):
    rp, d = ga.shape
    width = bs[0].shape[0]
    bfd = jax.ShapeDtypeStruct((rp, d), BF)
    low = jax.ShapeDtypeStruct((rp, width), BF)
    return pl.pallas_call(
        attn_bwd_kernel,
        out_shape=(bfd, bfd, bfd, low, low, low, jax.ShapeDtypeStruct((6 * width, d), BF)),
        in_specs=[SMEM] + [VMEM] * 12,
        out_specs=(VMEM,) * 7,
        compiler_params=params(48),
        cost_estimate=cost(25),
        name="attn_bwd",
    )(banks, *kept, ga, *bs)


def input_bwd_kernel(
    tok, g1, gmid, gq, gk, gv, uq, uk, uv, wq, wk, wv, aq, ak, av, inp_o, total
):
    rows, d = tok.shape
    total[...] = (
        (nt(gq[...], wq[...]) + nt(uq[...], aq[...]))
        + (nt(gk[...], wk[...]) + nt(uk[...], ak[...]))
        + (nt(gv[...], wv[...]) + nt(uv[...], av[...]))
    )
    whole = rows // 16 * 16
    for r, count in [(s, min(112, whole - s)) for s in range(0, whole, 112)] + (
        [(whole, rows - whole)] if rows > whole else []
    ):
        rs = slice(r, r + count)
        xhat, rstd = norm_parts(tok[rs, :].astype(F32))
        inp_o[rs, :] = gmid[rs, :] + norm_back(xhat, rstd, g1[...], total[rs, :])


def input_backward(tok, g1, gmid, grads, ws):
    rows, d = tok.shape
    return pl.pallas_call(
        input_bwd_kernel,
        out_shape=jax.ShapeDtypeStruct((rows, d), F32),
        in_specs=[VMEM] * 15,
        out_specs=VMEM,
        scratch_shapes=[pltpu.VMEM(gmid.shape, F32)],
        compiler_params=params(48),
        cost_estimate=cost(10),
        name="input_bwd",
    )(tok, g1, gmid, *grads, *ws)


def finish_kernel(qkv, outr, *outs):
    width, d = outs[1].shape
    experts = outs[9].shape[1]
    for i in range(4):
        src, base = (qkv, 2 * i * width) if i < 3 else (outr, 0)
        outs[2 * i][...] = jnp.transpose(src[base : base + width, :].astype(F32))
        outs[2 * i + 1][...] = src[base + width : base + 2 * width, :].astype(F32)
    outs[8][...] = jnp.transpose(outr[2 * width : 3 * width, :].astype(F32))
    rb = jnp.transpose(outr[3 * width : 3 * width + 16, 0:width].astype(F32))
    outs[9][...] = rb[:, 0:experts]


def finish(qkv, outr, width, experts):
    d = qkv.shape[1]
    tall = jax.ShapeDtypeStruct((d, width), F32)
    wide = jax.ShapeDtypeStruct((width, d), F32)
    return pl.pallas_call(
        finish_kernel,
        out_shape=(tall, wide) * 4 + (tall, jax.ShapeDtypeStruct((width, experts), F32)),
        in_specs=[VMEM] * 2,
        out_specs=(VMEM,) * 10,
        compiler_params=params(32),
        cost_estimate=cost(3),
        name="finish",
    )(qkv, outr)


def finish_experts_kernel(*refs):
    ins, (ua, ub, da, db) = refs[:-4], refs[-4:]
    d, width = ua.shape[1:]
    ff = ub.shape[2]
    for j, src in enumerate(ins):
        ua[j] = jnp.transpose(src[:, 0:d].astype(F32))
        ub[j] = src[:, d : d + ff].astype(F32)
        da[j] = jnp.transpose(src[:, d + ff : d + 2 * ff].astype(F32))
        db[j] = src[:, d + 2 * ff :].astype(F32)


def finish_experts(bufs, d, ff):
    n = len(bufs)
    width = bufs[0].shape[0]
    shapes = ((n, d, width), (n, width, ff), (n, ff, width), (n, width, d))
    return pl.pallas_call(
        finish_experts_kernel,
        out_shape=tuple(jax.ShapeDtypeStruct(s, F32) for s in shapes),
        in_specs=[VMEM] * n,
        out_specs=(VMEM,) * 4,
        compiler_params=params(32),
        cost_estimate=cost(5),
        name="finish_experts",
    )(*bufs)


def hop(x, axis, k):
    n = lax.axis_size(axis)
    return lax.ppermute(x, axis, [(i, i ^ k) for i in range(n)])


def bits(axis):
    n = lax.axis_size(axis)
    return [1 << i for i in range(n.bit_length() - 1)]


def add(a, b):
    return (a.astype(F32) + b.astype(F32)).astype(BF)


def part_of(terms, bit, flip):
    half = terms[0].shape[0] // 2
    start = (bit if not flip else 1 - bit) * half
    return sum(lax.dynamic_slice_in_dim(t, start, half, 0).astype(F32) for t in terms).astype(BF)


def reduce_step(terms, axis, k):
    bit = (lax.axis_index(axis) // k) % 2
    send = part_of(terms, bit, True)
    return send, part_of(terms, bit, False), hop(send, axis, k)


def gather_step(buf, axis, k, wait=None):
    bit = (lax.axis_index(axis) // k) % 2
    other = hop(buf, axis, k)
    other = other if wait is None else after(other, wait)
    return jnp.where(
        bit == 0,
        jnp.concatenate([buf, other], axis=0),
        jnp.concatenate([other, buf], axis=0),
    )


def after(x, *deps):
    return lax.optimization_barrier((x,) + deps)[0]


def gather4(x):
    near = hop(x, "expert", 1)
    far = hop(x, "expert", 2)
    return [x, near, far, hop(far, "expert", 1)]


def body(
    tokens, cotangent, bank_ids, routes, attn_gain, expert_gain, query_w, key_w, value_w, out_w,
    query_a, query_b, key_a, key_b, value_a, value_b, out_a, out_b, router_w, router_a, router_b,
    up_w, up_a, up_b, down_w, down_a, down_b,
):
    rows, d = tokens.shape
    rp = 32 * (-(-rows // 32))
    width = query_a.shape[1]
    local = up_w.shape[0]
    groups = lax.axis_size("expert")
    experts = local * groups
    cap = 13 * rows // (4 * experts)
    me = lax.axis_index("expert").astype(I32).reshape(1)
    cot = jnp.pad(cotangent, ((0, rp - rows), (0, 0)))
    cot1 = hop(cot, "expert", 1)
    cot2 = hop(cot, "expert", 2)
    meta = jnp.concatenate([routes.T, jnp.repeat(bank_ids, SEQ)[None, :]], axis=0)
    meta = jnp.pad(meta, ((0, 0), (0, rp - rows)), constant_values=-1)
    meta = jnp.stack(gather4(meta))
    tables = routing_tables(me, meta, local) + (meta,)
    g1 = attn_gain.reshape(1, d)
    g2 = expert_gain.reshape(1, d)
    kept = attn_forward(
        bank_ids, tokens, g1,
        (query_w, key_w, value_w, query_a, query_b, key_a, key_b, value_a, value_b),
    )
    n1, q, k, v, lq, lk, lv, att, lse = kept
    out_ws = (out_w, out_a, out_b, router_w.T, router_a, router_b.T)
    lo, mid, n2, lr, pt = out_forward(
        bank_ids, tokens, g2, after(att, tables[0]), out_ws, (cot1, cot2)
    )
    near1 = hop(n2, "expert", 1)
    far2 = hop(n2, "expert", 2)
    cot3 = hop(after(cot2, n2), "expert", 1)
    crows = [cot, cot1, cot2, cot3]
    ews = (up_w, up_a, up_b, down_w, down_a, down_b)
    common = (crows, ews, cap)
    nrows = [n2, near1, None, None]
    e0n = expert_call(0, (0, 1), me, tables, nrows, *common, None)
    far2 = after(far2, e0n[1])
    nrows = [n2, near1, far2, hop(far2, "expert", 1)]
    e0f = expert_call(0, (2, 3), me, tables, nrows, *common, e0n[0])
    dp_steps = [("dp", k) for k in bits("dp")]
    ex_steps = [("expert", k) for k in bits("expert")]
    send0, keep0, got0 = reduce_step([e0f[0]], *dp_steps[0])
    e1f = expert_call(
        1, (2, 3), after(me, e0f[1], send0), tables, nrows, *common, None, e0f[1:]
    )
    grow = add(e1f[1], hop(e1f[2], "expert", 1))
    mix = add(e1f[3], hop(e1f[4], "expert", 1))
    send0, keep0, got0 = reduce_step([keep0, after(got0, e1f[1])], *dp_steps[1])
    e1n = expert_call(
        1, (0, 1), after(me, grow, send0), tables, nrows, *common, e1f[0], e0n[1:]
    )
    near = e1n[1:]
    grow_far = hop(grow, "expert", 2)
    grow_near = hop(after(near[1], grow_far), "expert", 1)
    mix_far = hop(after(mix, near[0]), "expert", 2)
    send0, keep0, got0 = reduce_step([keep0, after(got0, near[0])], *dp_steps[2])
    send1, keep1, got1 = reduce_step([after(e1n[0], near[0])], *dp_steps[0])
    gmid, ga, outr = out_backward(
        bank_ids, cot, g2, (att, lo, mid, n2, lr, pt), out_ws,
        (near[0], after(grow_near, send0, send1), grow_far),
    )
    got0 = after(got0, gmid)
    for step in dp_steps[3:]:
        _, keep0, got0 = reduce_step([keep0, got0], *step)
    buf0 = add(keep0, got0)
    send1, keep1, got1 = reduce_step([keep1, after(got1, gmid)], *dp_steps[1])
    *grads, qkv = attn_backward(
        bank_ids, (n1, q, k, v, lq, lk, lv, lse), after(ga, buf0, send1),
        (query_b, key_b, value_b),
    )
    up_steps = dp_steps[::-1]
    buf0 = gather_step(buf0, *up_steps[0], wait=qkv)
    mix_near = hop(after(near[3], qkv), "expert", 1)
    got1 = after(got1, qkv)
    shares = lax.axis_size("dp") * groups
    used = qkv.shape[0]
    flat = jnp.concatenate([qkv, outr], axis=0)
    flat = jnp.pad(flat, ((0, -flat.shape[0] % shares), (0, 0)))
    _, keep, got = reduce_step([flat], *ex_steps[0])
    send, keep, got = reduce_step([keep, got], *ex_steps[1])
    input_grad = input_backward(
        tokens, g1, after(gmid, send), grads,
        (query_w, key_w, value_w, query_a, key_a, value_a),
    )
    got = after(got, input_grad)
    for step in up_steps[1:]:
        buf0 = gather_step(buf0, *step)
    for step in dp_steps[2:]:
        _, keep1, got1 = reduce_step([keep1, got1], *step)
    buf1 = add(keep1, got1)
    for step in ex_steps[2:] + dp_steps:
        _, keep, got = reduce_step([keep, got], *step)
    flat = add(keep, got)
    for step in up_steps:
        buf1 = gather_step(buf1, *step)
    for step in reversed(ex_steps + dp_steps):
        flat = gather_step(flat, *step)
    qkv, outr = flat[:used], flat[used:]
    mixed = mid[:rows] + (
        near[2][:rows].astype(F32) + mix_near[:rows].astype(F32) + mix_far[:rows].astype(F32)
    )
    small = finish(qkv, outr, width, experts)
    large = finish_experts((buf0, buf1), d, up_w.shape[2])
    return (mixed.astype(BF), input_grad, *small, *large)


def solution(mesh):
    split = P(("dp", "expert"), None)
    by_expert = P("expert", None, None)
    in_specs = (split, split, P(("dp", "expert")), split) + (P(),) * 17 + (by_expert,) * 6
    out_specs = (split, split) + (P(),) * 10 + (by_expert,) * 4
    return jax.shard_map(body, mesh=mesh, in_specs=in_specs, out_specs=out_specs, check_vma=False)
```

time: 515 us -> 392 us (0.76); the launches traced: 523 us -> 384 us
  starting transfers between devices: 112 us -> 40.2 us
  waiting for transfers between devices: 162 us -> 96.9 us
  Pallas kernels: 198 us -> 214 us
  other arithmetic: 18.1 us -> 8.42 us
  local copies, waits for them, and re-layouts: 30.2 us -> 22.5 us
    ppermute x46 -> x37, starting transfers between devices: 112 us -> 40.2 us  [hop(): return lax.ppermute(x, axis, [(i, i ^ k) for i in range(n)])]
    ppermute x46 -> x37, waiting for transfers between devices: 162 us -> 96.9 us  [hop(): return lax.ppermute(x, axis, [(i, i ^ k) for i in range(n)])]
    pallas_call x4 -> x10, Pallas kernels: 165 us -> 191 us  [the longest x4 129 us: expert_call(): pl.pallas_call(functools.partial(expert_kernel, cfg), out_shape=out_shape...]
    pallas_call x1, Pallas kernels: 31.9 us -> 22.6 us  [attn_forward(): pl.pallas_call(attn_fwd_kernel, out_shape=out_shape, in_specs=[SMEM] + [V...]
    unnamed x69 -> x132, local copies, waits for them, and re-layouts: 20.6 us -> 13.2 us
    transpose x3 -> x0, local copies, waits for them, and re-layouts: 5.18 us -> none  [the longest x1 3.26 us: body(): da = jnp.swapaxes(both[:, :, d + ff:d + 2 * ff], 1, 2)]
  transfers between devices with their start and end apart: 46 -> 37, of which waited for: 24 -> 14; matrix products, arithmetic and copies ran while one was open for 5% -> 3% of each run, Pallas kernels for 23% -> 45%
where the time goes in v2:
time: 392 us; the launch traced here: 384 us
  Pallas kernels  214 us (55%)
  waiting for transfers between devices  96.9 us (25%)
  starting transfers between devices  40.2 us (10%)
  local copies, waits for them, and re-layouts  22.5 us (6%)
  other arithmetic  8.42 us (2%)
    pallas_call x4, Pallas kernels, expert_call(): pl.pallas_call(functools.partial(expert_kernel, cfg), out_shape=out_shape...  129 us
    ppermute x37, waiting for transfers between devices, hop(): return lax.ppermute(x, axis, [(i, i ^ k) for i in range(n)])  96.9 us
    ppermute x37, starting transfers between devices, hop(): return lax.ppermute(x, axis, [(i, i ^ k) for i in range(n)])  40.2 us
    pallas_call x1, Pallas kernels, attn_backward(): pl.pallas_call(attn_bwd_kernel, out_shape=(bfd, bfd, bfd, low, low, low,...  22.6 us
    pallas_call x1, Pallas kernels, attn_forward(): pl.pallas_call(attn_fwd_kernel, out_shape=out_shape, in_specs=[SMEM] + [V...  22.6 us
    pallas_call x1, Pallas kernels, out_backward(): pl.pallas_call(out_bwd_kernel, out_shape=(jax.ShapeDtypeStruct((rp, d), F...  15.2 us
    unnamed x132, local copies, waits for them, and re-layouts  13.2 us
    pallas_call x1, Pallas kernels, input_backward(): pl.pallas_call(input_bwd_kernel, out_shape=jax.ShapeDtypeStruct((rows, d)...  9.1 us
  transfers between devices with their start and end apart: 37, of which 14 were waited for; matrix products, arithmetic and copies ran while one was open for 3% of the time, Pallas kernels for 45%

profile of v2, /device:TPU:0, one launch (start us, length us, event | category | flops | bytes accessed | tf_op | source)
XLA Modules:
  0.0 384.4 jit_solution(1785852049449274843)
XLA Ops:
  2.2 3.0 collective-permute-start.1
  5.2 1.4 pad.9.refs_5_.cot
  8.0 22.6 %attn_fwd.1 = (bf16[800,768]{1,0:T(8,128)(2,1)}, bf16[800,768]{1,0:T(8,128)(2,1)}, bf16[800,768]{1,0:T(8,128)(2,1)}, bf16[800,768]{1,0:T(8,128)(2,1)}, bf16[800,...) custom-call(s32[4]{0:T(128)} %banks.7, ...), custom_call_target="tpu_custom_call" | custom-call | flops 27499999232 | bytes 75000000 | tf_op jit(solution)/shard_map/attn_fwd/pallas_call | solution.py:238
  30.8 1.2 routing_tables.1
  32.7 3.5 collective-permute-done.4.rest_1_.refs_5_
  37.3 1.3 copy-done.11
  38.6 8.6 %out_fwd.1 = (bf16[800,128]{1,0:T(8,128)(2,1)S(1)}, f32[800,768]{1,0:T(8,128)S(1)}, bf16[848,768]{1,0:T(8,128)(2,1)S(1)}, bf16[800,128]{1,0:T(8,128)(2,1)S(1)}, f32[8,800]{1,0:T(8,128)S(1)}) custom-call(s32[4]{0:T(128)S(1)} %copy-done.6, bf16[788,768]{1,0:T(8,128)(2,1)S(1)} %copy-done.14, f32[1,768]{1,0:T(1,128)S(1)} %reshape.41.g2, ...), custom_call_target="tpu_custom_call" | custom-call | flops 9900000256 | bytes 27000000 | tf_op jit(solution)/shard_map/out_fwd/pallas_call | solution.py:261
  47.3 1.4 copy-done
  50.4 2.7 collective-permute-done.6.refs_4_
  53.1 29.2 %expert0_near.1 = (f32[128,7680]{1,0:T(8,128)}, bf16[960,768]{1,0:T(8,128)(2,1)S(1)}, bf16[960,768]{1,0:T(8,128)(2,1)S(1)}, f32[2,800]{1,0:T(2,128)S(1)}) custom-call(s32[1]{0:T(128)} %bitcast.eidx.refs_0_, f32[8,800]{1,0:T(8,128)S(1)} %get-tuple-element.94.refs_1_, s32[4,3,800]{2,1,0:T(4,128)S(1)} %pad_add_fusion.routes.refs_2_, ...), custom_call_target="tpu_custom_call" | custom-call | flops 32999999488 | bytes 90000000 | tf_op jit(solution)/shard_map/expert0_near/pallas_call | solution.py:517
  83.5 1.1 copy-done.48
  85.7 4.5 %collective-permute-done.8.refs_6_ = bf16[800,768]{1,0:T(8,128)(2,1)S(1)} collective-permute-done((bf16[800,768]{1,0:T(8,128)(2,1)}, bf16[800,768]{1,0:T(8,128)(2,1)S(1)}, u32[]{:S(2)}, u32[]{:S(2)}) %collective-permute-start.8) | collective-permute-done | bytes 1228832 | tf_op jit(solution)/shard_map/ppermute | solution.py:750
  90.2 32.6 %expert0_far.1 = (f32[128,7680]{1,0:T(8,128)}, bf16[960,768]{1,0:T(8,128)(2,1)S(1)}, bf16[960,768]{1,0:T(8,128)(2,1)S(1)}, f32[2,800]{1,0:T(2,128)S(1)}) custom-call(s32[1]{0:T(128)} %bitcast.eidx.refs_0_, f32[8,800]{1,0:T(8,128)S(1)} %get-tuple-element.94.refs_1_, s32[4,3,800]{2,1,0:T(4,128)S(1)} %pad_add_fusion.routes.refs_2_, ...), custom_call_target="tpu_custom_call" | custom-call | flops 32999999488 | bytes 90000000 | tf_op jit(solution)/shard_map/expert0_far/pallas_call | solution.py:517
  123.4 3.4 dynamic-slice_convert_fusion.2
  126.9 1.5 collective-permute-start.10
  128.4 28.0 %expert1_far.1 = (f32[128,7680]{1,0:T(8,128)}, bf16[832,768]{1,0:T(8,128)(2,1)}, bf16[832,768]{1,0:T(8,128)(2,1)}, bf16[800,768]{1,0:T(8,128)(2,1)}, bf16[800,768]{1,0:T(8,128)(2,1)}) custom-call(s32[1]{0:T(128)} %bitcast.eidx.refs_0_, f32[8,800]{1,0:T(8,128)} %copy-done.42, s32[4,3,800]{2,1,0:T(4,128)} %copy-done.4, ...), custom_call_target="tpu_custom_call" | custom-call | flops 32999999488 | bytes 90000000 | tf_op jit(solution)/shard_map/expert1_far/pallas_call | solution.py:517
  156.4 10.9 %collective-permute-start.9 = (bf16[832,768]{1,0:T(8,128)(2,1)}, bf16[832,768]{1,0:T(8,128)(2,1)}, u32[]{:S(2)}, u32[]{:S(2)}) collective-permute-start(bf16[832,768]{1,0:T(8,128)(2,1)} %get-tuple-element.109), channel_id=1, source_target_pairs={{0,1},{1,0},{2,3},{3,2},{4,5},{5,4},{6,7},{7,6},{8,9},{9,8},{10,11... | collective-permute-start | bytes 3833864 | tf_op jit(solution)/shard_map/ppermute | solution.py:750
  167.9 2.4 collective-permute-done.9
  170.2 1.6 add_convert_fusion
  172.5 39.6 %expert1_near.1 = (f32[128,7680]{1,0:T(8,128)}, bf16[832,768]{1,0:T(8,128)(2,1)}, bf16[832,768]{1,0:T(8,128)(2,1)}, bf16[800,768]{1,0:T(8,128)(2,1)}, bf16[800,768]{1,0:T(8,128)(2,1)}) custom-call(s32[1]{0:T(128)} %bitcast.eidx.refs_0_, f32[8,800]{1,0:T(8,128)} %copy-done.42, s32[4,3,800]{2,1,0:T(4,128)} %copy-done.4, bf16[848,768]{1,0:T(8,128)(2,1)} %copy-done.7, ...), custom_call_target="tpu_custom_call" | custom-call | flops 32999999488 | bytes 90000000 | tf_op jit(solution)/shard_map/expert1_near/pallas_call | solution.py:517
  212.3 2.9 dynamic-slice_convert_fusion
  215.9 2.6 collective-permute-start.14
  219.6 15.2 %out_bwd.1 = (f32[800,768]{1,0:T(8,128)}, bf16[800,768]{1,0:T(8,128)(2,1)S(1)}, bf16[416,768]{1,0:T(8,128)(2,1)S(1)}) custom-call(s32[4]{0:T(128)S(1)} %copy-done.6, bf16[800,768]{1,0:T(8,128)(2,1)S(1)} %copy-done.3, f32[1,768]{1,0:T(1,128)S(1)} %reshape.41.g2, bf16[800,768]{1,0:T(8,128)(2,1)} %get-tuple-element.95.att, bf16[800,128]{1,0:T(8,128)(2,1)S(1)} %copy-done.44, ...), custom_call_target="tpu_custom_call" | custom-call | flops 15399999488 | bytes 42000000 | tf_op jit(solution)/shard_map/out_bwd/pallas_call | solution.py:570
  234.8 4.0 %collective-permute-done.15 = bf16[64,7680]{1,0:T(8,128)(2,1)S(1)} collective-permute-done((bf16[64,7680]{1,0:T(8,128)(2,1)S(1)}, bf16[64,7680]{1,0:T(8,128)(2,1)S(1)}, u32[]{:S(2)}, u32[]{:S(2)}) %collective-permute-start.15) | collective-permute-done | bytes 983072 | tf_op jit(solution)/shard_map/ppermute | solution.py:750
  239.2 1.4 collective-permute-start.32
  240.7 1.6 collective-permute-start.29
  242.4 22.6 %attn_bwd.1 = (bf16[800,768]{1,0:T(8,128)(2,1)S(1)}, bf16[800,768]{1,0:T(8,128)(2,1)S(1)}, bf16[800,768]{1,0:T(8,128)(2,1)}, bf16[800,128]{1,0:T(8,128)(2,1)S(1)...) custom-call(s32[4]{0:T(128)S(1)} %copy-done.6, ...), custom_call_target="tpu_custom_call" | custom-call | flops 27499999232 | bytes 75000000 | tf_op jit(solution)/shard_map/attn_bwd/pallas_call | solution.py:652
  267.5 1.8 collective-permute-start.18
  270.3 1.3 collective-permute-start.20
  271.6 9.1 %input_bwd.1 = f32[788,768]{1,0:T(8,128)} custom-call(bf16[788,768]{1,0:T(8,128)(2,1)S(1)} %copy-done.15, f32[1,768]{1,0:T(1,128)S(1)} %copy-done.5, f32[800,768]{1,0:T(8,128)} %get-tuple-element.146.gmid, bf16[800,768]{1,0:T(8,128)(2,1)} %copy-done.38, bf16[800,768]{1,0:T(8,128)(2,1)} %copy-done.39, bf16[800,768]{1,0:T(8,128)(2,1)} %get-tuple-element.149.gv, ...), custom_call_target="tpu_custom_call" | custom-call | flops 11000000512 | bytes 30000000 | tf_op jit(solution)/shard_map/input_bwd/pallas_call | solution.py:683
  280.8 25.5 %collective-permute-done.20 = bf16[296,768]{1,0:T(8,128)(2,1)S(1)} collective-permute-done((bf16[296,768]{1,0:T(8,128)(2,1)S(1)}, bf16[296,768]{1,0:T(8,128)(2,1)S(1)}, u32[]{:S(2)}, u32[]{:S(2)}) %collective-permute-start.20) | collective-permute-done | bytes 454688 | tf_op jit(solution)/shard_map/ppermute | solution.py:750
  306.5 1.8 collective-permute-start.21
  308.4 1.5 collective-permute-start.30
  309.9 3.3 collective-permute-done.21
  313.4 1.9 collective-permute-start.22
  315.6 12.7 %collective-permute-done.22 = bf16[74,768]{1,0:T(8,128)(2,1)S(1)} collective-permute-done((bf16[74,768]{1,0:T(8,128)(2,1)S(1)}, bf16[74,768]{1,0:T(8,128)(2,1)S(1)}, u32[]{:S(2)}, u32[]{:S(2)}) %collective-permute-start.22) | collective-permute-done | bytes 113696 | tf_op jit(solution)/shard_map/ppermute | solution.py:750
  329.0 4.6 %collective-permute-done.23 = bf16[37,768]{1,0:T(8,128)(2,1)S(1)} collective-permute-done((bf16[37,768]{1,0:T(8,128)(2,1)S(1)}, bf16[37,768]{1,0:T(8,128)(2,1)S(1)}, u32[]{:S(2)}, u32[]{:S(2)}) %collective-permute-start.23) | collective-permute-done | bytes 56864 | tf_op jit(solution)/shard_map/ppermute | solution.py:750
  333.8 2.1 collective-permute-start.35
  335.9 3.1 collective-permute-done.24
  339.2 1.6 add_convert_fusion.2
  340.9 7.9 %collective-permute-done.25 = bf16[74,768]{1,0:T(8,128)(2,1)S(1)} collective-permute-done((bf16[74,768]{1,0:T(8,128)(2,1)S(1)}, bf16[74,768]{1,0:T(8,128)(2,1)S(1)}, u32[]{:S(2)}, u32[]{:S(2)}) %collective-permute-start.25) | collective-permute-done | bytes 113696 | tf_op jit(solution)/shard_map/ppermute | solution.py:750
  349.4 1.8 collective-permute-start.36
  351.2 6.4 %collective-permute-done.26 = bf16[148,768]{1,0:T(8,128)(2,1)S(1)} collective-permute-done((bf16[148,768]{1,0:T(8,128)(2,1)S(1)}, bf16[148,768]{1,0:T(8,128)(2,1)S(1)}, u32[]{:S(2)}, u32[]{:S(2)}) %collective-permute-start.26) | collective-permute-done | bytes 227360 | tf_op jit(solution)/shard_map/ppermute | solution.py:750
  357.7 1.6 collective-permute-start.27
  359.6 6.6 %collective-permute-done.27 = bf16[296,768]{1,0:T(8,128)(2,1)S(1)} collective-permute-done((bf16[296,768]{1,0:T(8,128)(2,1)S(1)}, bf16[296,768]{1,0:T(8,128)(2,1)S(1)}, u32[]{:S(2)}, u32[]{:S(2)}) %collective-permute-start.27) | collective-permute-done | bytes 454688 | tf_op jit(solution)/shard_map/ppermute | solution.py:750
  366.6 9.7 %collective-permute-done.36 = bf16[64,7680]{1,0:T(8,128)(2,1)S(1)} collective-permute-done((bf16[64,7680]{1,0:T(8,128)(2,1)S(1)}, bf16[64,7680]{1,0:T(8,128)(2,1)S(1)}, u32[]{:S(2)}, u32[]{:S(2)}) %collective-permute-start.36) | collective-permute-done | bytes 983072 | tf_op jit(solution)/shard_map/ppermute | solution.py:750
  376.7 3.7 finish_experts.1
  381.2 2.1 finish.1
  (209 shorter events, 21.5 us)
Async XLA Ops:
  2.2 5.7 %collective-permute-start.1 = (s32[3,800]{1,0:T(4,128)S(1)}, s32[3,800]{1,0:T(4,128)S(1)}, u32[]{:S(2)}, u32[]{:S(2)}) collective-permute-start(s32[3,800]{1,0:T(4,128)S(1)} %get-tuple-element.201), channel_id=1, source_target_pairs={{0,2},{1,3},{2,0},{3,1},{4,6},{5,7},{6,4},{7,5},{8,10},{9,11},{10,... | collective-permute-start | bytes 28808 | tf_op jit(solution)/shard_map/ppermute | solution.py:750
  5.2 25.4 %collective-permute-start = (s32[3,800]{1,0:T(4,128)S(1)}, s32[3,800]{1,0:T(4,128)S(1)}, u32[]{:S(2)}, u32[]{:S(2)}) collective-permute-start(s32[3,800]{1,0:T(4,128)S(1)} %get-tuple-element.201), channel_id=1, source_target_pairs={{0,1},{1,0},{2,3},{3,2},{4,5},{5,4},{6,7},{7,6},{8,9},{9,8},{10,11... | collective-permute-start | bytes 28808 | tf_op jit(solution)/shard_map/ppermute | solution.py:750
  6.6 46.5 %copy-start.2 = (bf16[800,768]{1,0:T(8,128)(2,1)}, bf16[800,768]{1,0:T(8,128)(2,1)S(1)}, u32[]{:S(2)}) copy-start(bf16[800,768]{1,0:T(8,128)(2,1)S(1)} %pad.9.refs_5_.cot) | copy-start | bytes 3686404
  6.6 29.6 %collective-permute-start.4 = (bf16[800,768]{1,0:T(8,128)(2,1)S(1)}, bf16[800,768]{1,0:T(8,128)(2,1)}, u32[]{:S(2)}, u32[]{:S(2)}) collective-permute-start(bf16[800,768]{1,0:T(8,128)(2,1)S(1)} %pad.9.refs_5_.cot), channel_id=1, source_target_pairs={{0,2},{1,3},{2,0},{3,1},{4,6},{5,7},{6,4},{7,5},{8,10},{9,11},{10,... | collective-permute-start | bytes 3686408 | tf_op jit(solution)/shard_map/ppermute | solution.py:750
  6.8 29.4 %collective-permute-start.3 = (bf16[800,768]{1,0:T(8,128)(2,1)S(1)}, bf16[800,768]{1,0:T(8,128)(2,1)S(1)}, u32[]{:S(2)}, u32[]{:S(2)}) collective-permute-start(bf16[800,768]{1,0:T(8,128)(2,1)S(1)} %pad.9.refs_5_.cot), channel_id=1, source_target_pairs={{0,1},{1,0},{2,3},{3,2},{4,5},{5,4},{6,7},{7,6},{8,9},{9,8},{10,11... | collective-permute-start | bytes 3686408 | tf_op jit(solution)/shard_map/ppermute | solution.py:750
  7.9 22.8 %copy-start.61 = (f32[768]{0:T(1024)S(1)}, f32[768]{0:T(1024)}, u32[]{:S(2)}) copy-start(f32[768]{0:T(1024)} %param.32) | copy-start | bytes 9220
  7.9 22.8 %collective-permute-start.2 = (s32[3,800]{1,0:T(4,128)S(1)}, s32[3,800]{1,0:T(4,128)S(1)}, u32[]{:S(2)}, u32[]{:S(2)}) collective-permute-start(s32[3,800]{1,0:T(4,128)S(1)} %collective-permute-done.1), channel_id=1, source_target_pairs={{0,1},{1,0},{2,3},{3,2},{4,5},{5,4},{6,7},{7,6},{8,9},{9,8},{10,11... | collective-permute-start | bytes 28808 | tf_op jit(solution)/shard_map/ppermute | solution.py:750
  30.7 59.5 %copy-start.4 = (s32[4,3,800]{2,1,0:T(4,128)}, s32[4,3,800]{2,1,0:T(4,128)S(1)}, u32[]{:S(2)}) copy-start(s32[4,3,800]{2,1,0:T(4,128)S(1)} %pad_add_fusion.routes.refs_2_) | copy-start | bytes 115204
  38.6 14.5 %copy-start.21 = (bf16[2,768,128]{2,1,0:T(8,128)(2,1)S(1)}, bf16[2,768,128]{2,1,0:T(8,128)(2,1)}, u32[]{:S(2)}) copy-start(bf16[2,768,128]{2,1,0:T(8,128)(2,1)} %refs_8_.7) | copy-start | bytes 1179652
  38.6 14.5 %copy-start.22 = (bf16[2,128,768]{2,1,0:T(8,128)(2,1)S(1)}, bf16[2,128,768]{2,1,0:T(8,128)(2,1)}, u32[]{:S(2)}) copy-start(bf16[2,128,768]{2,1,0:T(8,128)(2,1)} %refs_12_.7) | copy-start | bytes 1179652
  50.1 32.3 %copy-start.7 = (bf16[848,768]{1,0:T(8,128)(2,1)}, bf16[848,768]{1,0:T(8,128)(2,1)S(1)}, u32[]{:S(2)}) copy-start(bf16[848,768]{1,0:T(8,128)(2,1)S(1)} %get-tuple-element.97.refs_3_.n2) | copy-start | bytes 3907588
  50.1 3.0 collective-permute-start.6
  50.1 35.1 %collective-permute-start.5 = (bf16[848,768]{1,0:T(8,128)(2,1)S(1)}, bf16[848,768]{1,0:T(8,128)(2,1)}, u32[]{:S(2)}, u32[]{:S(2)}) collective-permute-start(bf16[848,768]{1,0:T(8,128)(2,1)S(1)} %get-tuple-element.97.refs_3_.n2), channel_id=1, source_target_pairs={{0,2},{1,3},{2,0},{3,1},{4,6},{5,7},{6,4},{7,5},{8,10},{9,11},{10,... | collective-permute-start | bytes 3907592 | tf_op jit(solution)/shard_map/ppermute | solution.py:750
  53.1 29.3 %copy-start.8 = (bf16[848,768]{1,0:T(8,128)(2,1)}, bf16[848,768]{1,0:T(8,128)(2,1)S(1)}, u32[]{:S(2)}) copy-start(bf16[848,768]{1,0:T(8,128)(2,1)S(1)} %collective-permute-done.6.refs_4_) | copy-start | bytes 3907588
  85.2 5.0 %collective-permute-start.7 = (bf16[848,768]{1,0:T(8,128)(2,1)}, bf16[848,768]{1,0:T(8,128)(2,1)S(1)}, u32[]{:S(2)}, u32[]{:S(2)}) collective-permute-start(bf16[848,768]{1,0:T(8,128)(2,1)} %collective-permute-done.5.refs_3_), channel_id=1, source_target_pairs={{0,1},{1,0},{2,3},{3,2},{4,5},{5,4},{6,7},{7,6},{8,9},{9,8},{10,11... | collective-permute-start | bytes 3907592 | tf_op jit(solution)/shard_map/ppermute | solution.py:750
  85.3 4.9 %collective-permute-start.8 = (bf16[800,768]{1,0:T(8,128)(2,1)}, bf16[800,768]{1,0:T(8,128)(2,1)S(1)}, u32[]{:S(2)}, u32[]{:S(2)}) collective-permute-start(bf16[800,768]{1,0:T(8,128)(2,1)} %collective-permute-done.4.rest_1_.refs_5_), channel_id=1, source_target_pairs={{0,1},{1,0},{2,3},{3,2},{4,5},{5,4},{6,7},{7,6},{8,9},{9,8},{10,11... | collective-permute-start | bytes 3686408 | tf_op jit(solution)/shard_map/ppermute | solution.py:750
  90.2 32.6 %copy-start.13 = (bf16[800,768]{1,0:T(8,128)(2,1)}, bf16[800,768]{1,0:T(8,128)(2,1)S(1)}, u32[]{:S(2)}) copy-start(bf16[800,768]{1,0:T(8,128)(2,1)S(1)} %collective-permute-done.8.refs_6_) | copy-start | bytes 3686404
  90.2 32.6 %copy-start.9 = (bf16[848,768]{1,0:T(8,128)(2,1)}, bf16[848,768]{1,0:T(8,128)(2,1)S(1)}, u32[]{:S(2)}) copy-start(bf16[848,768]{1,0:T(8,128)(2,1)S(1)} %collective-permute-done.7.refs_4_) | copy-start | bytes 3907588
  126.9 40.7 %collective-permute-start.10 = (bf16[64,7680]{1,0:T(8,128)(2,1)S(1)}, bf16[64,7680]{1,0:T(8,128)(2,1)S(1)}, u32[]{:S(2)}, u32[]{:S(2)}) collective-permute-start(bf16[64,7680]{1,0:T(8,128)(2,1)S(1)} %get-tuple-element.189), channel_id=1, source_target_pairs={{0,4},{4,0},{8,12},{12,8},{16,20},{20,16},{24,28},{28,24},{1,5},{5... | collective-permute-start | bytes 2949128 | tf_op jit(solution)/shard_map/ppermute | solution.py:750
  156.4 13.8 %collective-permute-start.9 = (bf16[832,768]{1,0:T(8,128)(2,1)}, bf16[832,768]{1,0:T(8,128)(2,1)}, u32[]{:S(2)}, u32[]{:S(2)}) collective-permute-start(bf16[832,768]{1,0:T(8,128)(2,1)} %get-tuple-element.109), channel_id=1, source_target_pairs={{0,1},{1,0},{2,3},{3,2},{4,5},{5,4},{6,7},{7,6},{8,9},{9,8},{10,11... | collective-permute-start | bytes 3833864 | tf_op jit(solution)/shard_map/ppermute | solution.py:750
  167.3 99.3 %collective-permute-start.17 = (bf16[800,768]{1,0:T(8,128)(2,1)}, bf16[800,768]{1,0:T(8,128)(2,1)S(1)}, u32[]{:S(2)}, u32[]{:S(2)}) collective-permute-start(bf16[800,768]{1,0:T(8,128)(2,1)} %get-tuple-element.143), channel_id=1, source_target_pairs={{0,1},{1,0},{2,3},{3,2},{4,5},{5,4},{6,7},{7,6},{8,9},{9,8},{10,11... | collective-permute-start | bytes 3686408 | tf_op jit(solution)/shard_map/ppermute | solution.py:750
  167.8 48.0 %collective-permute-start.13 = (bf16[32,7680]{1,0:T(8,128)(2,1)S(1)}, bf16[32,7680]{1,0:T(8,128)(2,1)S(1)}, u32[]{:S(2)}, u32[]{:S(2)}) collective-permute-start(bf16[32,7680]{1,0:T(8,128)(2,1)S(1)} %get-tuple-element.195), channel_id=1, source_target_pairs={{0,8},{4,12},{8,0},{12,4},{16,24},{20,28},{24,16},{28,20},{1,9},{5... | collective-permute-start | bytes 1474568 | tf_op jit(solution)/shard_map/ppermute | solution.py:750
  171.9 40.2 %collective-permute-start.11 = (bf16[832,768]{1,0:T(8,128)(2,1)S(1)}, bf16[832,768]{1,0:T(8,128)(2,1)S(1)}, u32[]{:S(2)}, u32[]{:S(2)}) collective-permute-start(bf16[832,768]{1,0:T(8,128)(2,1)S(1)} %add_convert_fusion), channel_id=1, source_target_pairs={{0,2},{1,3},{2,0},{3,1},{4,6},{5,7},{6,4},{7,5},{8,10},{9,11},{10,... | collective-permute-start | bytes 3833864 | tf_op jit(solution)/shard_map/ppermute | solution.py:750
  212.2 6.3 %collective-permute-start.12 = (bf16[832,768]{1,0:T(8,128)(2,1)}, bf16[832,768]{1,0:T(8,128)(2,1)S(1)}, u32[]{:S(2)}, u32[]{:S(2)}) collective-permute-start(bf16[832,768]{1,0:T(8,128)(2,1)} %get-tuple-element.130), channel_id=1, source_target_pairs={{0,1},{1,0},{2,3},{3,2},{4,5},{5,4},{6,7},{7,6},{8,9},{9,8},{10,11... | collective-permute-start | bytes 3833864 | tf_op jit(solution)/shard_map/ppermute | solution.py:750
  215.2 23.7 %collective-permute-start.15 = (bf16[64,7680]{1,0:T(8,128)(2,1)S(1)}, bf16[64,7680]{1,0:T(8,128)(2,1)S(1)}, u32[]{:S(2)}, u32[]{:S(2)}) collective-permute-start(bf16[64,7680]{1,0:T(8,128)(2,1)S(1)} %get-tuple-element.187), channel_id=1, source_target_pairs={{0,4},{4,0},{8,12},{12,8},{16,20},{20,16},{24,28},{28,24},{1,5},{5... | collective-permute-start | bytes 2949128 | tf_op jit(solution)/shard_map/ppermute | solution.py:750
  215.9 23.0 %collective-permute-start.14 = (bf16[16,7680]{1,0:T(8,128)(2,1)S(1)}, bf16[16,7680]{1,0:T(8,128)(2,1)S(1)}, u32[]{:S(2)}, u32[]{:S(2)}) collective-permute-start(bf16[16,7680]{1,0:T(8,128)(2,1)S(1)} %add_convert_fusion.14), channel_id=1, source_target_pairs={{0,16},{4,20},{8,24},{12,28},{16,0},{20,4},{24,8},{28,12},{1,17},{... | collective-permute-start | bytes 737288 | tf_op jit(solution)/shard_map/ppermute | solution.py:750
  239.2 30.1 %collective-permute-start.32 = (bf16[32,7680]{1,0:T(8,128)(2,1)S(1)}, bf16[32,7680]{1,0:T(8,128)(2,1)S(1)}, u32[]{:S(2)}, u32[]{:S(2)}) collective-permute-start(bf16[32,7680]{1,0:T(8,128)(2,1)S(1)} %get-tuple-element.193), channel_id=1, source_target_pairs={{0,8},{4,12},{8,0},{12,4},{16,24},{20,28},{24,16},{28,20},{1,9},{5... | collective-permute-start | bytes 1474568 | tf_op jit(solution)/shard_map/ppermute | solution.py:750
  240.7 28.6 %collective-permute-start.29 = (bf16[16,7680]{1,0:T(8,128)(2,1)S(1)}, bf16[16,7680]{1,0:T(8,128)(2,1)S(1)}, u32[]{:S(2)}, u32[]{:S(2)}) collective-permute-start(bf16[16,7680]{1,0:T(8,128)(2,1)S(1)} %add_convert_fusion.12), channel_id=1, source_target_pairs={{0,16},{4,20},{8,24},{12,28},{16,0},{20,4},{24,8},{28,12},{1,17},{... | collective-permute-start | bytes 737288 | tf_op jit(solution)/shard_map/ppermute | solution.py:750
  266.5 3.5 collective-permute-start.19
  267.5 71.6 %collective-permute-start.18 = (bf16[800,768]{1,0:T(8,128)(2,1)S(1)}, bf16[800,768]{1,0:T(8,128)(2,1)S(1)}, u32[]{:S(2)}, u32[]{:S(2)}) collective-permute-start(bf16[800,768]{1,0:T(8,128)(2,1)S(1)} %add_convert_fusion.1), channel_id=1, source_target_pairs={{0,2},{1,3},{2,0},{3,1},{4,6},{5,7},{6,4},{7,5},{8,10},{9,11},{10,... | collective-permute-start | bytes 3686408 | tf_op jit(solution)/shard_map/ppermute | solution.py:750
  269.3 69.9 %collective-permute-start.16 = (bf16[800,768]{1,0:T(8,128)(2,1)S(1)}, bf16[800,768]{1,0:T(8,128)(2,1)S(1)}, u32[]{:S(2)}, u32[]{:S(2)}) collective-permute-start(bf16[800,768]{1,0:T(8,128)(2,1)S(1)} %copy-done.64), channel_id=1, source_target_pairs={{0,1},{1,0},{2,3},{3,2},{4,5},{5,4},{6,7},{7,6},{8,9},{9,8},{10,11... | collective-permute-start | bytes 3686408 | tf_op jit(solution)/shard_map/ppermute | solution.py:750
  269.4 45.8 %collective-permute-start.33 = (bf16[16,7680]{1,0:T(8,128)(2,1)S(1)}, bf16[16,7680]{1,0:T(8,128)(2,1)S(1)}, u32[]{:S(2)}, u32[]{:S(2)}) collective-permute-start(bf16[16,7680]{1,0:T(8,128)(2,1)S(1)} %add_convert_fusion.10), channel_id=1, source_target_pairs={{0,16},{4,20},{8,24},{12,28},{16,0},{20,4},{24,8},{28,12},{1,17},{... | collective-permute-start | bytes 737288 | tf_op jit(solution)/shard_map/ppermute | solution.py:750
  270.3 35.9 %collective-permute-start.20 = (bf16[296,768]{1,0:T(8,128)(2,1)S(1)}, bf16[296,768]{1,0:T(8,128)(2,1)S(1)}, u32[]{:S(2)}, u32[]{:S(2)}) collective-permute-start(bf16[296,768]{1,0:T(8,128)(2,1)S(1)} %get-tuple-element.191), channel_id=1, source_target_pairs={{0,2},{1,3},{2,0},{3,1},{4,6},{5,7},{6,4},{7,5},{8,10},{9,11},{10,... | collective-permute-start | bytes 1363976 | tf_op jit(solution)/shard_map/ppermute | solution.py:750
  306.5 6.7 %collective-permute-start.21 = (bf16[148,768]{1,0:T(8,128)(2,1)S(1)}, bf16[148,768]{1,0:T(8,128)(2,1)S(1)}, u32[]{:S(2)}, u32[]{:S(2)}) collective-permute-start(bf16[148,768]{1,0:T(8,128)(2,1)S(1)} %get-tuple-element.197), channel_id=1, source_target_pairs={{0,4},{4,0},{8,12},{12,8},{16,20},{20,16},{24,28},{28,24},{1,5},{5... | collective-permute-start | bytes 681992 | tf_op jit(solution)/shard_map/ppermute | solution.py:750
  308.4 20.1 %collective-permute-start.30 = (bf16[32,7680]{1,0:T(8,128)(2,1)S(1)}, bf16[32,7680]{1,0:T(8,128)(2,1)S(1)}, u32[]{:S(2)}, u32[]{:S(2)}) collective-permute-start(bf16[32,7680]{1,0:T(8,128)(2,1)S(1)} %maximum_select_fusion.6), channel_id=1, source_target_pairs={{0,8},{4,12},{8,0},{12,4},{16,24},{20,28},{24,16},{28,20},{1,9},{5... | collective-permute-start | bytes 1474568 | tf_op jit(solution)/shard_map/ppermute | solution.py:750
  313.4 15.0 %collective-permute-start.22 = (bf16[74,768]{1,0:T(8,128)(2,1)S(1)}, bf16[74,768]{1,0:T(8,128)(2,1)S(1)}, u32[]{:S(2)}, u32[]{:S(2)}) collective-permute-start(bf16[74,768]{1,0:T(8,128)(2,1)S(1)} %get-tuple-element.199), channel_id=1, source_target_pairs={{0,8},{4,12},{8,0},{12,4},{16,24},{20,28},{24,16},{28,20},{1,9},{5... | collective-permute-start | bytes 341000 | tf_op jit(solution)/shard_map/ppermute | solution.py:750
  315.3 24.0 %copy-start.59 = (bf16[800,768]{1,0:T(8,128)(2,1)S(1)}, bf16[800,768]{1,0:T(8,128)(2,1)}, u32[]{:S(2)}) copy-start(bf16[800,768]{1,0:T(8,128)(2,1)} %get-tuple-element.115) | copy-start | bytes 3686404
  315.4 23.9 %copy-start.1 = (f32[800,768]{1,0:T(8,128)S(1)}, f32[800,768]{1,0:T(8,128)}, u32[]{:S(2)}) copy-start(f32[800,768]{1,0:T(8,128)} %copy-done) | copy-start | bytes 7372804
  315.4 18.3 %collective-permute-start.34 = (bf16[16,7680]{1,0:T(8,128)(2,1)S(1)}, bf16[16,7680]{1,0:T(8,128)(2,1)S(1)}, u32[]{:S(2)}, u32[]{:S(2)}) collective-permute-start(bf16[16,7680]{1,0:T(8,128)(2,1)S(1)} %add_convert_fusion.9), channel_id=1, source_target_pairs={{0,16},{4,20},{8,24},{12,28},{16,0},{20,4},{24,8},{28,12},{1,17},{... | collective-permute-start | bytes 737288 | tf_op jit(solution)/shard_map/ppermute | solution.py:750
  328.4 5.2 %collective-permute-start.23 = (bf16[37,768]{1,0:T(8,128)(2,1)S(1)}, bf16[37,768]{1,0:T(8,128)(2,1)S(1)}, u32[]{:S(2)}, u32[]{:S(2)}) collective-permute-start(bf16[37,768]{1,0:T(8,128)(2,1)S(1)} %add_convert_fusion.20), channel_id=1, source_target_pairs={{0,16},{4,20},{8,24},{12,28},{16,0},{20,4},{24,8},{28,12},{1,17},{... | collective-permute-start | bytes 170504 | tf_op jit(solution)/shard_map/ppermute | solution.py:750
  328.6 30.7 %collective-permute-start.31 = (bf16[64,7680]{1,0:T(8,128)(2,1)S(1)}, bf16[64,7680]{1,0:T(8,128)(2,1)S(1)}, u32[]{:S(2)}, u32[]{:S(2)}) collective-permute-start(bf16[64,7680]{1,0:T(8,128)(2,1)S(1)} %maximum_select_fusion.3), channel_id=1, source_target_pairs={{0,4},{4,0},{8,12},{12,8},{16,20},{20,16},{24,28},{28,24},{1,5},{5... | collective-permute-start | bytes 2949128 | tf_op jit(solution)/shard_map/ppermute | solution.py:750
  333.6 5.5 %collective-permute-start.24 = (bf16[37,768]{1,0:T(8,128)(2,1)S(1)}, bf16[37,768]{1,0:T(8,128)(2,1)S(1)}, u32[]{:S(2)}, u32[]{:S(2)}) collective-permute-start(bf16[37,768]{1,0:T(8,128)(2,1)S(1)} %add_convert_fusion.19), channel_id=1, source_target_pairs={{0,16},{4,20},{8,24},{12,28},{16,0},{20,4},{24,8},{28,12},{1,17},{... | collective-permute-start | bytes 170504 | tf_op jit(solution)/shard_map/ppermute | solution.py:750
  333.8 15.4 %collective-permute-start.35 = (bf16[32,7680]{1,0:T(8,128)(2,1)S(1)}, bf16[32,7680]{1,0:T(8,128)(2,1)S(1)}, u32[]{:S(2)}, u32[]{:S(2)}) collective-permute-start(bf16[32,7680]{1,0:T(8,128)(2,1)S(1)} %maximum_select_fusion.7), channel_id=1, source_target_pairs={{0,8},{4,12},{8,0},{12,4},{16,24},{20,28},{24,16},{28,20},{1,9},{5... | collective-permute-start | bytes 1474568 | tf_op jit(solution)/shard_map/ppermute | solution.py:750
  339.1 9.6 %collective-permute-start.25 = (bf16[74,768]{1,0:T(8,128)(2,1)S(1)}, bf16[74,768]{1,0:T(8,128)(2,1)S(1)}, u32[]{:S(2)}, u32[]{:S(2)}) collective-permute-start(bf16[74,768]{1,0:T(8,128)(2,1)S(1)} %maximum_select_fusion.10), channel_id=1, source_target_pairs={{0,8},{4,12},{8,0},{12,4},{16,24},{20,28},{24,16},{28,20},{1,9},{5... | collective-permute-start | bytes 341000 | tf_op jit(solution)/shard_map/ppermute | solution.py:750
  348.8 8.7 %collective-permute-start.26 = (bf16[148,768]{1,0:T(8,128)(2,1)S(1)}, bf16[148,768]{1,0:T(8,128)(2,1)S(1)}, u32[]{:S(2)}, u32[]{:S(2)}) collective-permute-start(bf16[148,768]{1,0:T(8,128)(2,1)S(1)} %maximum_select_fusion.9), channel_id=1, source_target_pairs={{0,4},{4,0},{8,12},{12,8},{16,20},{20,16},{24,28},{28,24},{1,5},{5... | collective-permute-start | bytes 681992 | tf_op jit(solution)/shard_map/ppermute | solution.py:750
  349.4 26.9 %collective-permute-start.36 = (bf16[64,7680]{1,0:T(8,128)(2,1)S(1)}, bf16[64,7680]{1,0:T(8,128)(2,1)S(1)}, u32[]{:S(2)}, u32[]{:S(2)}) collective-permute-start(bf16[64,7680]{1,0:T(8,128)(2,1)S(1)} %maximum_select_fusion.4), channel_id=1, source_target_pairs={{0,4},{4,0},{8,12},{12,8},{16,20},{20,16},{24,28},{28,24},{1,5},{5... | collective-permute-start | bytes 2949128 | tf_op jit(solution)/shard_map/ppermute | solution.py:750
  357.7 8.5 %collective-permute-start.27 = (bf16[296,768]{1,0:T(8,128)(2,1)S(1)}, bf16[296,768]{1,0:T(8,128)(2,1)S(1)}, u32[]{:S(2)}, u32[]{:S(2)}) collective-permute-start(bf16[296,768]{1,0:T(8,128)(2,1)S(1)} %maximum_select_fusion.8), channel_id=1, source_target_pairs={{0,2},{1,3},{2,0},{3,1},{4,6},{5,7},{6,4},{7,5},{8,10},{9,11},{10,... | collective-permute-start | bytes 1363976 | tf_op jit(solution)/shard_map/ppermute | solution.py:750
  366.6 13.8 %collective-permute-start.28 = (bf16[592,768]{1,0:T(8,128)(2,1)S(1)}, bf16[592,768]{1,0:T(8,128)(2,1)S(1)}, u32[]{:S(2)}, u32[]{:S(2)}) collective-permute-start(bf16[592,768]{1,0:T(8,128)(2,1)S(1)} %maximum_select_fusion.5), channel_id=1, source_target_pairs={{0,1},{1,0},{2,3},{3,2},{4,5},{5,4},{6,7},{7,6},{8,9},{9,8},{10,11... | collective-permute-start | bytes 2727944 | tf_op jit(solution)/shard_map/ppermute | solution.py:750
  (54 other events, 229.0 us)
